TPU v7x, 256 devices: a whole 4x4x8 slice. The times are simulated.
256 devices in a mesh: dp: 16 (over z_lo, y, core), expert: 16 (over z_hi, x).
Axes of the slice: x: 4, y: 4, z: 8 (z_hi: 4, z_lo: 2; z = z_hi * 2 + z_lo), core: 2. Of those that a mesh axis runs over, the one named last changes fastest.
Arguments:
- quant_rows: bfloat16 [32768, 3584], P(('dp', 'expert')), may hold values from -6 to 6
- row_scales: bfloat16 [32768, 28], P(('dp', 'expert')), may hold values from 0.25 to 4
- out_grad: bfloat16 [32768, 3584], P(('dp', 'expert')), may hold values from -6 to 6
- combine: bfloat16 [32768, 8], P(('dp', 'expert')), may hold values from 0.049804688 to 1
- expert_ids: int32 [32768, 8], P(('dp', 'expert')), may hold values from 0 to 255, all different within a row
- gate_w: bfloat16 [16, 4096, 3584], P('expert', 'dp'), may hold values from -0.09375 to 0.09375
- up_w: bfloat16 [16, 4096, 3584], P('expert', 'dp'), may hold values from -0.09375 to 0.09375
- down_w: bfloat16 [16, 4096, 3584], P('expert', 'dp'), may hold values from -0.125 to 0.125
Outputs:
- in_grad: bfloat16 [32768, 3584], P(('dp', 'expert'))
- combine_grad: bfloat16 [32768, 8], P(('dp', 'expert'))
- gate_w_grad: bfloat16 [16, 4096, 3584], P('expert', 'dp')
- up_w_grad: bfloat16 [16, 4096, 3584], P('expert', 'dp')
- down_w_grad: bfloat16 [16, 4096, 3584], P('expert', 'dp')
Inputs may be any that keep to these rules, and one draw needn't show every extreme that they name: `expert_ids`: each row names 8 different experts.
All inputs are finite; a program needn't handle non-finite values.
Results may differ from a plain program's by a relative error of at most 0.02.
Values may be sent and summed in bfloat16 or wider, within the bound.
No kernel may reach another device: no remote copies, remote signals or barrier semaphores. Data moves between devices by JAX's collectives and lax.ppermute only.
A program may use at most 128 MiB of HBM per device.

v0:
```python
import jax
import jax.numpy as jnp
from jax import lax
from jax.sharding import PartitionSpec as P

EXP_DEV = 16
CAP = 2


rows_pair = (((0,), (0,)), ((), ()))
last_pair = (((1,), (1,)), ((), ()))


def dequantize(quant_rows, row_scales):
    count_rows = quant_rows.shape[0]
    blocks = (
        quant_rows.astype(jnp.float32).reshape(count_rows, -1, 128)
        * row_scales.astype(jnp.float32)[:, :, None]
    )
    return blocks.reshape(count_rows, -1).astype(jnp.bfloat16)


def local_work(slot_x, slot_scales, slot_dy, slot_weight, gate_rows, up_rows, down_rows):
    count_rows = slot_x.shape[0] * slot_x.shape[1]
    width = slot_x.shape[2]
    rows_x = dequantize(slot_x.reshape(count_rows, width), slot_scales.reshape(count_rows, -1))
    rows_dy = slot_dy.reshape(count_rows, width)
    weight = slot_weight.reshape(count_rows, 1).astype(jnp.float32)
    h_gate = lax.dot_general(rows_x, gate_rows, last_pair, preferred_element_type=jnp.float32)
    h_up = lax.dot_general(rows_x, up_rows, last_pair, preferred_element_type=jnp.float32)
    sig = jax.nn.sigmoid(h_gate)
    act = h_gate * sig * h_up
    back = lax.dot_general(rows_dy, down_rows, last_pair, preferred_element_type=jnp.float32)
    gate_part = jnp.sum(act * back, axis=1)
    scaled = (weight * rows_dy.astype(jnp.float32)).astype(jnp.bfloat16)
    grad_down = lax.dot_general(
        act.astype(jnp.bfloat16), scaled, rows_pair, preferred_element_type=jnp.float32
    )
    d_act = weight * back
    dh_up = (d_act * h_gate * sig).astype(jnp.bfloat16)
    dh_gate = (d_act * h_up * sig * (1.0 + h_gate * (1.0 - sig))).astype(jnp.bfloat16)
    grad_gate = lax.dot_general(dh_gate, rows_x, rows_pair, preferred_element_type=jnp.float32)
    grad_up = lax.dot_general(dh_up, rows_x, rows_pair, preferred_element_type=jnp.float32)
    partial_value = jnp.dot(dh_gate, gate_rows, preferred_element_type=jnp.float32)
    partial_value = partial_value + jnp.dot(dh_up, up_rows, preferred_element_type=jnp.float32)
    return (grad_gate, grad_up, grad_down, partial_value, gate_part)


def body(quant_rows, row_scales, out_grad, combine, expert_ids, gate_w, up_w, down_w):
    tok_count = quant_rows.shape[0]
    top_count = expert_ids.shape[1]
    width = quant_rows.shape[1]
    expert_count = lax.axis_size("expert")
    dp_count = lax.axis_size("dp")
    half_count = dp_count // 2
    window = 2 * expert_count
    slot_total = window * CAP
    source_count = dp_count * expert_count
    gate_rows = gate_w[0]
    up_rows = up_w[0]
    down_rows = down_w[0]
    own_half = lax.axis_index("dp") // half_count
    targets = jnp.arange(window, dtype=jnp.int32) * (EXP_DEV // 2)
    route_hits = (expert_ids.reshape(-1)[:, None] == targets[None, :]).astype(jnp.int32)
    route_rank = jnp.cumsum(route_hits, axis=0) - 1
    route_kept = route_hits * (route_rank < CAP).astype(jnp.int32)
    route_live = jnp.sum(route_kept, axis=1) > 0
    expert_of = jnp.sum(route_kept * jnp.arange(window, dtype=jnp.int32)[None, :], axis=1)
    rank_of = jnp.sum(route_kept * route_rank, axis=1)
    route_slot = jnp.where(route_live, expert_of * CAP + rank_of, -1)
    route_sel = (route_slot[:, None] == jnp.arange(slot_total, dtype=jnp.int32)[None, :]).astype(
        jnp.bfloat16
    )
    token_sel = jnp.sum(
        route_sel.reshape(tok_count, top_count, slot_total).astype(jnp.float32), axis=1
    ).astype(jnp.bfloat16)
    send_x = lax.dot_general(
        token_sel, quant_rows, rows_pair, preferred_element_type=jnp.float32
    ).astype(jnp.bfloat16)
    send_scales = lax.dot_general(
        token_sel, row_scales, rows_pair, preferred_element_type=jnp.float32
    ).astype(jnp.bfloat16)
    send_dy = lax.dot_general(
        token_sel, out_grad, rows_pair, preferred_element_type=jnp.float32
    ).astype(jnp.bfloat16)
    send_weight = lax.dot_general(
        route_sel, combine.reshape(-1), rows_pair, preferred_element_type=jnp.float32
    ).astype(jnp.bfloat16)
    send_x = send_x.reshape(expert_count, 2, CAP, width)
    send_scales = send_scales.reshape(expert_count, 2, CAP, -1)
    send_dy = send_dy.reshape(expert_count, 2, CAP, width)
    send_weight = send_weight.reshape(expert_count, 2, CAP)
    recv_x, recv_scales = (
        lax.all_to_all(send_x, "expert", split_axis=0, concat_axis=0, tiled=True),
        lax.all_to_all(send_scales, "expert", split_axis=0, concat_axis=0, tiled=True),
    )
    recv_dy, recv_weight = (
        lax.all_to_all(send_dy, "expert", split_axis=0, concat_axis=0, tiled=True),
        lax.all_to_all(send_weight, "expert", split_axis=0, concat_axis=0, tiled=True),
    )
    whole_x, whole_scales, whole_dy, whole_weight = (
        lax.all_gather(recv_x, "dp", axis=0, tiled=True),
        lax.all_gather(recv_scales, "dp", axis=0, tiled=True),
        lax.all_gather(recv_dy, "dp", axis=0, tiled=True),
        lax.all_gather(recv_weight, "dp", axis=0, tiled=True),
    )
    mine_x = lax.dynamic_index_in_dim(whole_x, own_half, 1, keepdims=False)
    mine_scales = lax.dynamic_index_in_dim(whole_scales, own_half, 1, keepdims=False)
    mine_dy = lax.dynamic_index_in_dim(whole_dy, own_half, 1, keepdims=False)
    mine_weight = lax.dynamic_index_in_dim(whole_weight, own_half, 1, keepdims=False)
    grad_gate, grad_up, grad_down, partial_value, gate_part = local_work(
        mine_x, mine_scales, mine_dy, mine_weight, gate_rows, up_rows, down_rows
    )
    keep = jnp.arange(2, dtype=jnp.int32) == own_half
    full_rows = jnp.where(
        keep[None, :, None, None],
        partial_value.reshape(source_count, 1, CAP, width),
        jnp.float32(0.0),
    )
    full_gate = jnp.where(
        keep[None, :, None], gate_part.reshape(source_count, 1, CAP), jnp.float32(0.0)
    )
    slot_rows, gate_sums = (
        lax.psum_scatter(
            full_rows.astype(jnp.bfloat16), "dp", scatter_dimension=0, tiled=True
        ).astype(jnp.float32),
        lax.psum_scatter(
            full_gate.astype(jnp.bfloat16), "dp", scatter_dimension=0, tiled=True
        ).astype(jnp.float32),
    )
    back_rows = slot_rows.astype(jnp.bfloat16).reshape(expert_count, 2 * CAP, width)
    back_gate = gate_sums.astype(jnp.bfloat16).reshape(expert_count, 2 * CAP)
    home_rows, home_gate = (
        lax.all_to_all(back_rows, "expert", split_axis=0, concat_axis=0, tiled=True),
        lax.all_to_all(back_gate, "expert", split_axis=0, concat_axis=0, tiled=True),
    )
    in_grad = jnp.dot(
        token_sel, home_rows.reshape(slot_total, width), preferred_element_type=jnp.float32
    ).astype(jnp.bfloat16)
    combine_grad = jnp.dot(
        route_sel, home_gate.reshape(slot_total), preferred_element_type=jnp.float32
    )
    combine_grad = combine_grad.astype(jnp.bfloat16).reshape(tok_count, top_count)
    return (
        in_grad,
        combine_grad,
        grad_gate.astype(jnp.bfloat16)[None],
        grad_up.astype(jnp.bfloat16)[None],
        grad_down.astype(jnp.bfloat16)[None],
    )


def solution(mesh):
    return jax.shard_map(
        body,
        mesh=mesh,
        in_specs=(
            P(("dp", "expert"), None),
            P(("dp", "expert"), None),
            P(("dp", "expert"), None),
            P(("dp", "expert"), None),
            P(("dp", "expert"), None),
            P("expert", "dp", None),
            P("expert", "dp", None),
            P("expert", "dp", None),
        ),
        out_specs=(
            P(("dp", "expert"), None),
            P(("dp", "expert"), None),
            P("expert", "dp", None),
            P("expert", "dp", None),
            P("expert", "dp", None),
        ),
        check_vma=False,
    )
```

profile of v0, /device:TPU:24, one launch (start us, length us, event | category | flops | bytes accessed | tf_op | source)
XLA Modules:
  0.0 442.5 jit_solution(4780995901980100666)
XLA Ops:
  8.4 9.0 %reduce-window.6 = s32[32,8,128]{2,1,0:T(8,128)S(1)} reduce-window(s32[32,8,128]{2,1,0:T(8,128)S(1)} %compare_convert_fusion, s32[]{:T(128)} %constant.44.clone.1), window={size=1x1x128 pad=0_0x0_0x127_0}, to_apply=%region_0.1 | reduce-window | flops 4161536 | bytes 262148 | tf_op jit(solution)/shard_map/reduce-window
  19.9 26.5 %all_to_all.34 = bf16[16,2,2,3584]{3,2,1,0:T(2,128)(2,1)} all-to-all(bf16[16,2,2,3584]{3,2,1,0:T(2,128)(2,1)S(1)} %reshape.170), channel_id=1, replica_groups=mesh['dp'=16,'expert'=16] {'expert'}, dimensions={0} | all-to-all | bytes 917504 | tf_op jit(solution)/shard_map/all_to_all | solution.py:94
  48.1 25.6 %all_to_all.35 = bf16[16,2,2,3584]{3,2,1,0:T(2,128)(2,1)} all-to-all(bf16[16,2,2,3584]{3,2,1,0:T(2,128)(2,1)S(1)} %reshape.168), channel_id=1, replica_groups=mesh['dp'=16,'expert'=16] {'expert'}, dimensions={0} | all-to-all | bytes 917504 | tf_op jit(solution)/shard_map/all_to_all | solution.py:98
  75.1 3.5 all-to-all-start
  79.5 9.0 %all-to-all-done = bf16[16,2,2]{2,1,0:T(2,128)(2,1)S(1)} async-done(((bf16[16,2,2]{2,1,0:T(2,128)(2,1)}), bf16[16,2,2]{2,1,0:T(2,128)(2,1)S(1)}, u32[]{:S(2)}, u32[]{:S(2)}) %all-to-all-start) | async-done | bytes 160 | tf_op jit(solution)/shard_map/all_to_all | solution.py:99
  88.5 3.5 all-to-all-start.3
  92.0 15.7 %all_gather.12 = bf16[256,2,2]{2,1,0:T(2,128)(2,1)S(1)} all-gather(bf16[16,2,2]{2,1,0:T(2,128)(2,1)S(1)} %all-to-all-done), channel_id=1, replica_groups=mesh['dp'=16,'expert'=16] {'dp'}, dimensions={0}, use_global_device_ids=true | all-gather | bytes 2176 | tf_op jit(solution)/shard_map/all_gather | solution.py:105
  108.3 20.3 %all_gather.15 = bf16[256,2,2,28]{3,2,1,0:T(2,128)(2,1)S(1)} all-gather(bf16[16,2,2,28]{3,2,1,0:T(2,128)(2,1)S(1)} %all-to-all-done.3), channel_id=1, replica_groups=mesh['dp'=16,'expert'=16] {'dp'}, dimensions={0}, use_global_device_ids=true | all-gather | bytes 60928 | tf_op jit(solution)/shard_map/all_gather | solution.py:103
  128.7 7.6 %dynamic-slice_convert_fusion = f32[256,1,2,3584]{3,2,1,0:T(2,128)} fusion(bf16[256,2,2,3584]{3,2,1,0:T(2,128)(2,1)} %all-gather.5.cloned.1.call-done, s32[]{:T(128)S(6)} %select_n.37), kind=kLoop, calls=%fused_computation.15 | loop fusion | flops 1835008 | bytes 11010052 | tf_op jit(solution)/shard_map/convert_element_type | solution.py:17
  136.3 11.1 %reshape.177 = f32[512,28,128]{2,1,0:T(8,128)} reshape(f32[256,1,2,3584]{3,2,1,0:T(2,128)} %dynamic-slice_convert_fusion) | data formatting | bytes 14680064 | tf_op jit(solution)/shard_map/convert_element_type | solution.py:17
  147.4 7.8 %multiply_convert_fusion = bf16[512,28,128]{2,1,0:T(8,128)(2,1)} fusion(f32[512,28,128]{2,1,0:T(8,128)} %reshape.177, f32[512,28]{1,0:T(8,128)S(1)} %convert.5), kind=kLoop, calls=%fused_computation.1 | loop fusion | flops 3670016 | bytes 11067392 | tf_op jit(solution)/shard_map/convert_element_type | solution.py:20
  155.2 7.4 %copy.72 = bf16[512,28,128]{0,2,1:T(8,128)(2,1)} copy(bf16[512,28,128]{2,1,0:T(8,128)(2,1)} %multiply_convert_fusion) | data formatting | bytes 7340032 | tf_op jit(solution)/shard_map/convert_element_type | solution.py:20
  162.6 3.8 fusion.9
  166.5 1.9 fusion.6
  168.4 6.3 %constant_dynamic-slice_fusion = bf16[256,1,2,3584]{3,2,1,0:T(2,128)(2,1)} fusion(bf16[256,2,2,3584]{3,2,1,0:T(2,128)(2,1)} %all-gather.3.cloned.1.call-done, s32[]{:T(128)S(6)} %select_n.37), kind=kLoop, calls=%fused_computation.53 | loop fusion | bytes 7340036 | tf_op jit(solution)/shard_map/jit(dynamic_index_in_dim)/dynamic_slice | solution.py:109
  174.8 8.4 %reshape.169 = bf16[512,3584]{1,0:T(8,128)(2,1)} reshape(bf16[256,1,2,3584]{3,2,1,0:T(2,128)(2,1)} %constant_dynamic-slice_fusion) | data formatting | bytes 7340032 | tf_op jit(solution)/shard_map/reshape | solution.py:27
  183.2 4.0 multiply_reduce_fusion
  188.7 3.1 convolution_add_fusion
  191.8 8.1 %broadcast_in_dim.66 = bf16[256,2,3584]{2,1,0:T(2,128)(2,1)} reshape(bf16[512,3584]{1,0:T(8,128)(2,1)} %convolution_add_fusion) | data formatting | bytes 7340032 | tf_op jit(solution)/shard_map/jit(_where)/broadcast_in_dim | solution.py:115
  201.1 9.7 %select_convert_fusion = bf16[256,2,2,3584]{3,2,1,0:T(2,128)(2,1)} fusion(pred[2]{0:T(512)(128)(4,1)S(1)} %iota_compare_fusion.4, bf16[256,2,3584]{2,1,0:T(2,128)(2,1)} %broadcast_in_dim.66), kind=kLoop, calls=%fused_computation | loop fusion | flops 3670016 | bytes 11010050 | tf_op jit(solution)/shard_map/convert_element_type | solution.py:125
  212.8 3.9 mul.115.clone
  216.7 8.5 %copy.76 = f32[512,3584]{1,0:T(8,128)} copy(f32[512,3584]{0,1:T(8,128)} %bitcast.87) | data formatting | bytes 14680064 | tf_op jit(solution)/shard_map/mul | solution.py:17
  225.2 9.6 %reshape.179 = f32[512,3584]{1,0:T(8,128)} reshape(f32[256,1,2,3584]{3,2,1,0:T(2,128)} %dynamic-slice_convert_fusion) | data formatting | bytes 14680064 | tf_op jit(solution)/shard_map/convert_element_type | solution.py:17
  234.8 6.2 %multiply_convert_fusion.2 = bf16[512,3584]{1,0:T(8,128)(2,1)S(1)} fusion(f32[512,3584]{1,0:T(8,128)} %reshape.179, f32[512,3584]{1,0:T(8,128)} %copy.76), kind=kLoop, calls=%fused_computation.3 | loop fusion | flops 3670016 | bytes 18350080 | tf_op jit(solution)/shard_map/convert_element_type | solution.py:20
  242.8 2.3 fusion
  245.1 16.6 %reduce-scatter.4.cloned.1.call-done = bf16[16,4]{1,0:T(8,128)(2,1)} async-done(((bf16[256,4]{1,0:T(8,128)(2,1)}), bf16[16,4]{1,0:T(8,128)(2,1)}) %reduce-scatter.4.cloned.1.call-update) | async-done | bytes 144
  263.1 9.4 %all-to-all-start.5 = ((bf16[16,1,4]{2,1,0:T(2,128)(2,1)}), bf16[16,1,4]{2,1,0:T(2,128)(2,1)S(1)}, u32[]{:S(2)}, u32[]{:S(2)}) async-start(bf16[16,1,4]{2,1,0:T(2,128)(2,1)} %copy.74), calls=%async_computation.5 | async-start | bytes 16384 | tf_op jit(solution)/shard_map/all_to_all | solution.py:135
  272.5 134.2 %all-reduce.3.cloned.1.call-done = bf16[256,2,2,3584]{3,2,1,0:T(2,128)(2,1)} async-done(((bf16[256,2,2,3584]{3,2,1,0:T(2,128)(2,1)}), bf16[256,2,2,3584]{3,2,1,0:T(2,128)(2,1)}) %all-reduce.3.cloned.1.call-update) | async-done | bytes 7340048
  409.0 9.5 %all-to-all-start.4 = ((bf16[16,4,3584]{2,1,0:T(4,128)(2,1)}), bf16[16,4,3584]{2,1,0:T(4,128)(2,1)S(1)}, u32[]{:S(2)}, u32[]{:S(2)}) async-start(bf16[16,4,3584]{2,1,0:T(4,128)(2,1)} %reshape.172), calls=%async_computation.4 | async-start | bytes 917504 | tf_op jit(solution)/shard_map/all_to_all | solution.py:134
  418.5 4.5 %fusion.1 = bf16[1,256,3584]{2,1,0:T(8,128)(2,1)} fusion(bf16[512,256]{0,1:T(8,128)(2,1)S(1)} %get-tuple-element.35, bf16[512,3584]{1,0:T(8,128)(2,1)} %copy-done.2), kind=kOutput, calls=%fused_computation.9 | convolution fusion | flops 940441600 | bytes 5767168 | tf_op jit(solution)/shard_map/dot_general | solution.py:43
  423.0 3.6 fusion.2
  427.9 6.6 %all-to-all-done.4 = bf16[16,4,3584]{2,1,0:T(4,128)(2,1)S(1)} async-done(((bf16[16,4,3584]{2,1,0:T(4,128)(2,1)}), bf16[16,4,3584]{2,1,0:T(4,128)(2,1)S(1)}, u32[]{:S(2)}, u32[]{:S(2)}) %all-to-all-start.4) | async-done | bytes 458784 | tf_op jit(solution)/shard_map/all_to_all | solution.py:134
  (81 shorter events, 20.5 us)
Async XLA Ops:
  7.2 159.3 %copy-start = (bf16[1,256,3584]{2,1,0:T(8,128)(2,1)S(1)}, bf16[1,256,3584]{2,1,0:T(8,128)(2,1)}, u32[]{:S(2)}) copy-start(bf16[1,256,3584]{2,1,0:T(8,128)(2,1)} %param.13) | copy-start | bytes 5505028
  7.2 121.5 %all-gather.5.cloned.1.call-start = ((), (), s32[]{:S(2)}) async-start(), calls=%async_computation.8 | async-start | bytes 7798784 | tf_op jit(solution)/shard_map/all_gather | solution.py:102
  18.3 55.5 %copy-start.7 = (bf16[128,8]{0,1:T(8,128)(2,1)S(1)}, bf16[128,8]{0,1:T(8,128)(2,1)}, u32[]{:S(2)}) copy-start(bf16[128,8]{0,1:T(8,128)(2,1)} %param.11) | copy-start | bytes 6148
  18.3 60.4 %copy-start.6 = (bf16[128,28]{0,1:T(8,128)(2,1)S(1)}, bf16[128,28]{0,1:T(8,128)(2,1)}, u32[]{:S(2)}) copy-start(bf16[128,28]{0,1:T(8,128)(2,1)} %param.9) | copy-start | bytes 21508
  46.4 122.0 %all-gather.3.cloned.1.call-start = ((), (), s32[]{:S(2)}) async-start(), calls=%async_computation.7 | async-start | bytes 7798784 | tf_op jit(solution)/shard_map/all_gather | solution.py:104
  75.1 13.4 %all-to-all-start = ((bf16[16,2,2]{2,1,0:T(2,128)(2,1)}), bf16[16,2,2]{2,1,0:T(2,128)(2,1)S(1)}, u32[]{:S(2)}, u32[]{:S(2)}) async-start(bf16[16,2,2]{2,1,0:T(2,128)(2,1)} %reshape.167), calls=%async_computation | async-start | bytes 16384 | tf_op jit(solution)/shard_map/all_to_all | solution.py:99
  88.5 19.8 %all-to-all-start.3 = ((bf16[16,2,2,28]{3,2,1,0:T(2,128)(2,1)}), bf16[16,2,2,28]{3,2,1,0:T(2,128)(2,1)S(1)}, u32[]{:S(2)}, u32[]{:S(2)}) async-start(bf16[16,2,2,28]{3,2,1,0:T(2,128)(2,1)} %bitcast.4), calls=%async_computation.3 | async-start | bytes 32768 | tf_op jit(solution)/shard_map/all_to_all | solution.py:95
  92.0 169.7 %reduce-scatter.4.cloned.1.call-start = ((), (), s32[]{:S(2)}) async-start(), calls=%async_computation.9 | async-start | bytes 69632
  162.6 3.9 copy-start.4
  187.2 1.5 copy-start.5
  201.1 205.7 %all-reduce.3.cloned.1.call-start = ((), (), s32[]{:S(2)}) async-start(), calls=%async_computation.10 | async-start | bytes 14680064
  210.8 0.7 copy-start.8
  241.0 1.8 copy-start.2
  263.1 145.9 %all-to-all-start.5 = ((bf16[16,1,4]{2,1,0:T(2,128)(2,1)}), bf16[16,1,4]{2,1,0:T(2,128)(2,1)S(1)}, u32[]{:S(2)}, u32[]{:S(2)}) async-start(bf16[16,1,4]{2,1,0:T(2,128)(2,1)} %copy.74), calls=%async_computation.5 | async-start | bytes 16384 | tf_op jit(solution)/shard_map/all_to_all | solution.py:135
  409.0 25.5 %all-to-all-start.4 = ((bf16[16,4,3584]{2,1,0:T(4,128)(2,1)}), bf16[16,4,3584]{2,1,0:T(4,128)(2,1)S(1)}, u32[]{:S(2)}, u32[]{:S(2)}) async-start(bf16[16,4,3584]{2,1,0:T(4,128)(2,1)} %reshape.172), calls=%async_computation.4 | async-start | bytes 917504 | tf_op jit(solution)/shard_map/all_to_all | solution.py:134
  418.5 4.6 %copy-start.3 = (bf16[512,3584]{1,0:T(8,128)(2,1)S(1)}, bf16[512,3584]{1,0:T(8,128)(2,1)}, u32[]{:S(2)}) copy-start(bf16[512,3584]{1,0:T(8,128)(2,1)} %reshape.169) | copy-start | bytes 11010052
  418.5 17.5 %copy-start.1 = (bf16[1,256,3584]{2,1,0:T(8,128)(2,1)S(1)}, bf16[1,256,3584]{2,1,0:T(8,128)(2,1)}, u32[]{:S(2)}) copy-start(bf16[1,256,3584]{2,1,0:T(8,128)(2,1)} %param.13) | copy-start | bytes 5505028
Sparse Core Ops, SparseCore 0:
  46.6 53.8 all-gather.4
  102.3 51.5 all-gather.2
  201.2 60.4 reduce-scatter.3
  264.4 142.2 all-reduce.2
where the time goes:
time: 446 us; the launch traced here: 443 us
  waiting for transfers between devices  166 us (37%)
  blocking collectives  88.1 us (20%)
  local copies, waits for them, and re-layouts  76.4 us (17%)
  other arithmetic  41.3 us (9%)
  matrix products  29.6 us (7%)
  starting transfers between devices  26 us (6%)
  between operations  14.8 us (3%)
    unnamed x6, waiting for transfers between devices  151 us
    all_to_all x1, blocking collectives, body(): lax.all_to_all(send_x, 'expert', split_axis=0, concat_axis=0, tiled=True)  26.5 us
    all_to_all x1, blocking collectives, body(): lax.all_to_all(send_dy, 'expert', split_axis=0, concat_axis=0, tiled=True)  25.6 us
    convert_element_type x2, local copies, waits for them, and re-layouts, dequantize(): quant_rows.astype(jnp.float32).reshape(count_rows, -1, 128)  20.7 us
    all_gather x1, blocking collectives, body(): lax.all_gather(recv_scales, 'dp', axis=0, tiled=True)  20.3 us
    all_gather x1, blocking collectives, body(): lax.all_gather(recv_weight, 'dp', axis=0, tiled=True)  15.7 us
    convert_element_type x2, other arithmetic, dequantize(): return blocks.reshape(count_rows, -1).astype(jnp.bfloat16)  14 us
    mul x2, local copies, waits for them, and re-layouts, dequantize(): quant_rows.astype(jnp.float32).reshape(count_rows, -1, 128)  12.4 us
  transfers between devices with their start and end apart: 8, of which 4 were waited for; matrix products, arithmetic and copies ran while one was open for 22% of the time, Pallas kernels for 0%

commit v1 on v0

v1 whole, which is shorter than its diff:
```python
import jax
import jax.numpy as jnp
from jax import lax
from jax.sharding import Mesh, PartitionSpec as P

EXP_DEV = 16
CAP = 2
SCALE_BLOCK = 128
LANES = 128

rows_pair = (((0,), (0,)), ((), ()))
last_pair = (((1,), (1,)), ((), ()))

COLUMN = ("zlo", "zhi", "x")


def shift_y(value, step):
    count = lax.axis_size("y")
    return lax.ppermute(value, "y", [(i, (i + step) % count) for i in range(count)])


def swap_core(value):
    return lax.ppermute(value, "core", [(0, 1), (1, 0)])


def dequantize(quant_rows, row_scales):
    count_rows = quant_rows.shape[0]
    blocks = (
        quant_rows.astype(jnp.float32).reshape(count_rows, -1, SCALE_BLOCK)
        * row_scales.astype(jnp.float32)[:, :, None]
    )
    return blocks.reshape(count_rows, -1).astype(jnp.bfloat16)


def route(expert_ids, window):
    tok_count, top_count = expert_ids.shape
    slot_total = window * CAP
    column = jnp.arange(slot_total, dtype=jnp.int32)
    group = column // CAP
    rank = column % CAP
    half_window = window // 2
    target = (group % half_window) * EXP_DEV + (group // half_window) * (EXP_DEV // 2)
    hits = [
        (expert_ids[:, k : k + 1] == target[None, :]).astype(jnp.float32)
        for k in range(top_count)
    ]
    hit = sum(hits)
    before = jnp.tril(jnp.ones((tok_count, tok_count), jnp.float32), -1)
    place = jnp.dot(
        before.astype(jnp.bfloat16),
        hit.astype(jnp.bfloat16),
        preferred_element_type=jnp.float32,
    )
    kept = hit * (place == rank[None, :].astype(jnp.float32)).astype(jnp.float32)
    return hits, kept


def body(quant_rows, row_scales, out_grad, combine, expert_ids, gate_w, up_w, down_w):
    top_count = expert_ids.shape[1]
    width = quant_rows.shape[1]
    groups = lax.axis_size("zlo") * lax.axis_size("zhi") * lax.axis_size("x")
    hits, kept = route(expert_ids, groups)
    slots = groups * CAP
    kept_b = kept.astype(jnp.bfloat16)
    rows = dequantize(quant_rows, row_scales)
    weights = combine.astype(jnp.float32)
    slot_weight = sum(hits[k] * weights[:, k : k + 1] for k in range(top_count)) * kept
    slot_weight = jnp.sum(slot_weight, axis=0)
    pick = lambda v: lax.dot_general(
        kept_b, v, rows_pair, preferred_element_type=jnp.float32
    ).astype(jnp.bfloat16)
    tail = jnp.broadcast_to(slot_weight[:, None], (slots, LANES)).astype(jnp.bfloat16)
    send = jnp.concatenate([pick(rows), pick(out_grad), tail], axis=1)
    wide = send.shape[1]
    own = lax.all_to_all(
        send.reshape(groups, CAP, wide), COLUMN, split_axis=0, concat_axis=0, tiled=True
    ).reshape(slots, wide)

    half = slots // 2
    below = shift_y(own, 1)
    above = shift_y(own, -1)
    own_twin = swap_core(own)
    near = jnp.concatenate([below, above], axis=0)
    far_low = shift_y(below[:half], 1)
    far_high = shift_y(above[half:], -1)
    near_twin = swap_core(near)
    far = jnp.concatenate([far_low, far_high], axis=0)
    far_twin = swap_core(far)
    everything = jnp.concatenate(
        [own, near, far, own_twin, near_twin, far_twin], axis=0
    )
    x = everything[:, :width]
    dy = everything[:, width : 2 * width]
    weight = everything[:, 2 * width : 2 * width + 1].astype(jnp.float32)

    gate_rows = gate_w[0]
    up_rows = up_w[0]
    down_rows = down_w[0]
    h_gate = lax.dot_general(x, gate_rows, last_pair, preferred_element_type=jnp.float32)
    h_up = lax.dot_general(x, up_rows, last_pair, preferred_element_type=jnp.float32)
    sig = jax.nn.sigmoid(h_gate)
    act = h_gate * sig * h_up
    back = lax.dot_general(dy, down_rows, last_pair, preferred_element_type=jnp.float32)
    gate_part = jnp.sum(act * back, axis=1)
    scaled = (weight * dy.astype(jnp.float32)).astype(jnp.bfloat16)
    grad_down = lax.dot_general(
        act.astype(jnp.bfloat16), scaled, rows_pair, preferred_element_type=jnp.float32
    )
    d_act = weight * back
    dh_up = (d_act * h_gate * sig).astype(jnp.bfloat16)
    dh_gate = (d_act * h_up * sig * (1.0 + h_gate * (1.0 - sig))).astype(jnp.bfloat16)
    grad_gate = lax.dot_general(dh_gate, x, rows_pair, preferred_element_type=jnp.float32)
    grad_up = lax.dot_general(dh_up, x, rows_pair, preferred_element_type=jnp.float32)
    part = jnp.dot(dh_gate, gate_rows, preferred_element_type=jnp.float32)
    part = part + jnp.dot(dh_up, up_rows, preferred_element_type=jnp.float32)
    part = jnp.concatenate(
        [part, jnp.broadcast_to(gate_part[:, None], (part.shape[0], LANES))], axis=1
    )

    mine, other = part[: 4 * slots], part[4 * slots :]
    mine = mine + swap_core(other.astype(jnp.bfloat16)).astype(jnp.float32)
    s_own, s_below, s_above, s_far = (mine[k * slots : (k + 1) * slots] for k in range(4))
    far_b = s_far.astype(jnp.bfloat16)
    from_below = shift_y(far_b[:half], 1).astype(jnp.float32)
    from_above = shift_y(far_b[half:], -1).astype(jnp.float32)
    to_above = jnp.concatenate([s_above[:half] + from_below, s_above[half:]], axis=0)
    to_below = jnp.concatenate([s_below[:half], s_below[half:] + from_above], axis=0)
    total = (
        s_own
        + shift_y(to_above.astype(jnp.bfloat16), 1).astype(jnp.float32)
        + shift_y(to_below.astype(jnp.bfloat16), -1).astype(jnp.float32)
    ).astype(jnp.bfloat16)
    home = lax.all_to_all(
        total.reshape(groups, CAP, -1), COLUMN, split_axis=0, concat_axis=0, tiled=True
    ).reshape(slots, -1)
    in_grad = jnp.dot(kept_b, home[:, :width], preferred_element_type=jnp.float32).astype(
        jnp.bfloat16
    )
    slot_gate = home[:, width].astype(jnp.float32)[None, :] * kept
    combine_grad = jnp.stack(
        [jnp.sum(hits[k] * slot_gate, axis=1) for k in range(top_count)], axis=1
    ).astype(jnp.bfloat16)
    return (
        in_grad,
        combine_grad,
        grad_gate.astype(jnp.bfloat16)[None],
        grad_up.astype(jnp.bfloat16)[None],
        grad_down.astype(jnp.bfloat16)[None],
    )


def solution(mesh):
    fine = Mesh(
        mesh.devices.reshape(2, 4, 2, 4, 4), ("zlo", "y", "core", "zhi", "x")
    )
    tokens = P(("zlo", "y", "core", "zhi", "x"), None)
    hidden = P(("zhi", "x"), ("zlo", "y", "core"), None)
    return jax.shard_map(
        body,
        mesh=fine,
        in_specs=(tokens,) * 5 + (hidden,) * 3,
        out_specs=(tokens,) * 2 + (hidden,) * 3,
        check_vma=False,
    )
```

time: 446 us -> 149 us (0.33)
  waiting for transfers between devices: 166 us -> 52.8 us
  local copies, waits for them, and re-layouts: 76.4 us -> 11.4 us
  blocking collectives: 88.1 us -> 37.8 us
  other arithmetic: 41.3 us -> 3.27 us
  between operations: 14.8 us -> 0.96 us
  matrix products: 29.6 us -> 21.9 us
  starting transfers between devices: 26 us -> 20.1 us
    unnamed x6 -> x0, waiting for transfers between devices: 151 us -> none
    ppermute x0 -> x12, waiting for transfers between devices: none -> 51.2 us  [the longest x8 45.4 us: shift_y(): lax.ppermute(value, 'y', [(i, (i + step) % count) for i in range(count)])]
    all_gather x2 -> x0, blocking collectives: 35.9 us -> none  [the longest x1 20.3 us: body(): lax.all_gather(recv_scales, 'dp', axis=0, tiled=True)]
    convert_element_type x5 -> x0, local copies, waits for them, and re-layouts: 28.9 us -> none  [the longest x2 20.7 us: dequantize(): quant_rows.astype(jnp.float32).reshape(count_rows, -1, 128)]
    all_to_all x4 -> x1, starting transfers between devices: 25.8 us -> 8.82 us  [body(): lax.all_to_all(total.reshape(groups, CAP, -1), COLUMN, split_axis=0, conc...]
    convert_element_type x6 -> x4, other arithmetic: 17.9 us -> 0.97 us  [the longest x1 0.68 us: body(): weights = combine.astype(jnp.float32)]
    all_to_all x2 -> x1, blocking collectives: 52.1 us -> 37.8 us  [body(): lax.all_to_all(send.reshape(groups, CAP, wide), COLUMN, split_axis=0, con...]
    all_to_all x4 -> x1, waiting for transfers between devices: 15.6 us -> 1.61 us  [body(): lax.all_to_all(total.reshape(groups, CAP, -1), COLUMN, split_axis=0, conc...]
  transfers between devices with their start and end apart: 8 -> 13, of which waited for: 4 -> 9; matrix products, arithmetic and copies ran while one was open for 22% -> 10% of each run, Pallas kernels for 0% -> 0%
where the time goes in v1:
time: 149 us; the launch traced here: 148 us
  waiting for transfers between devices  52.8 us (35%)
  blocking collectives  37.8 us (25%)
  matrix products  21.9 us (15%)
  starting transfers between devices  20.1 us (13%)
  local copies, waits for them, and re-layouts  11.4 us (8%)
  other arithmetic  3.27 us (2%)
    ppermute x8, waiting for transfers between devices, shift_y(): lax.ppermute(value, 'y', [(i, (i + step) % count) for i in range(count)])  45.4 us
    all_to_all x1, blocking collectives, body(): lax.all_to_all(send.reshape(groups, CAP, wide), COLUMN, split_axis=0, con...  37.8 us
    ppermute x8, starting transfers between devices, shift_y(): lax.ppermute(value, 'y', [(i, (i + step) % count) for i in range(count)])  10.7 us
    all_to_all x1, starting transfers between devices, body(): lax.all_to_all(total.reshape(groups, CAP, -1), COLUMN, split_axis=0, conc...  8.82 us
    ppermute x4, waiting for transfers between devices, swap_core(): return lax.ppermute(value, 'core', [(0, 1), (1, 0)])  5.75 us
    dot_general x1, matrix products, body(): lax.dot_general(act.astype(jnp.bfloat16), scaled, rows_pair, preferred_el...  4.7 us
    unnamed x24, local copies, waits for them, and re-layouts  4.5 us
    dot_general x1, matrix products, body(): lax.dot_general(dh_gate, x, rows_pair, preferred_element_type=jnp.float32)  4.44 us
  transfers between devices with their start and end apart: 13, of which 9 were waited for; matrix products, arithmetic and copies ran while one was open for 10% of the time, Pallas kernels for 0%

profile of v1, /device:TPU:24, one launch (start us, length us, event | category | flops | bytes accessed | tf_op | source)
XLA Modules:
  0.0 148.2 jit_solution(14360294129356346294)
XLA Ops:
  0.7 1.0 slice_bitcast_fusion.15
  2.4 1.5 %copy.17 = bf16[128,3584]{0,1:T(8,128)(2,1)S(1)} copy(bf16[128,3584]{1,0:T(8,128)(2,1)} %param.8) | data formatting | bytes 1835008 | tf_op args[0]
  3.9 0.8 convert_element_type.138
  6.1 1.3 reshape.88
  7.4 37.8 %all_to_all.10 = bf16[32,2,7296]{2,1,0:T(2,128)(2,1)} all-to-all(bf16[32,2,7296]{2,1,0:T(2,128)(2,1)} %reshape.88), channel_id=1, replica_groups=mesh['zlo'=2,'y'=4,'core'=2,'zhi'=4,'x'=4] {'zlo','zhi','x'}, dimensions={0} | all-to-all | bytes 1867776 | tf_op jit(solution)/shard_map/all_to_all | solution.py:75
  45.2 2.5 %reshape.89 = bf16[64,7296]{1,0:T(8,128)(2,1)S(1)} reshape(bf16[32,2,7296]{2,1,0:T(2,128)(2,1)} %all_to_all.10) | data formatting | bytes 1867776 | tf_op jit(solution)/shard_map/reshape | solution.py:77
  48.0 1.8 %collective-permute-start.1 = (bf16[64,7296]{1,0:T(8,128)(2,1)S(1)}, bf16[64,7296]{1,0:T(8,128)(2,1)S(1)}, u32[]{:S(2)}, u32[]{:S(2)}) collective-permute-start(bf16[64,7296]{1,0:T(8,128)(2,1)S(1)} %reshape.89), channel_id=1, source_target_pairs={{0,96},{32,0},{64,32},{96,64},{1,97},{33,1},{65,33},{97,65},{2,98}... | collective-permute-start | bytes 2801672 | tf_op jit(solution)/shard_map/ppermute | solution.py:19
  49.9 18.7 %collective-permute-done = bf16[64,7296]{1,0:T(8,128)(2,1)S(1)} collective-permute-done((bf16[64,7296]{1,0:T(8,128)(2,1)S(1)}, bf16[64,7296]{1,0:T(8,128)(2,1)S(1)}, u32[]{:S(2)}, u32[]{:S(2)}) %collective-permute-start) | collective-permute-done | bytes 933920 | tf_op jit(solution)/shard_map/ppermute | solution.py:19
  68.6 0.8 collective-permute-start.2
  69.4 1.4 collective-permute-start.3
  71.3 6.5 %collective-permute-done.2 = bf16[32,7296]{1,0:T(8,128)(2,1)S(1)} collective-permute-done((bf16[32,7296]{1,0:T(8,128)(2,1)S(1)}, bf16[32,7296]{1,0:T(8,128)(2,1)S(1)}, u32[]{:S(2)}, u32[]{:S(2)}) %collective-permute-start.2) | collective-permute-done | bytes 466976 | tf_op jit(solution)/shard_map/ppermute | solution.py:19
  77.8 1.8 %collective-permute-done.3 = bf16[32,7296]{1,0:T(8,128)(2,1)S(1)} collective-permute-done((bf16[32,7296]{1,0:T(8,128)(2,1)S(1)}, bf16[32,7296]{1,0:T(8,128)(2,1)S(1)}, u32[]{:S(2)}, u32[]{:S(2)}) %collective-permute-start.3) | collective-permute-done | bytes 466976 | tf_op jit(solution)/shard_map/ppermute | solution.py:19
  80.4 2.0 %collective-permute-done.6 = bf16[64,7296]{1,0:T(8,128)(2,1)S(1)} collective-permute-done((bf16[64,7296]{1,0:T(8,128)(2,1)S(1)}, bf16[64,7296]{1,0:T(8,128)(2,1)S(1)}, u32[]{:S(2)}, u32[]{:S(2)}) %collective-permute-start.6) | collective-permute-done | bytes 933920 | tf_op jit(solution)/shard_map/ppermute | solution.py:23
  82.6 1.1 fusion.12
  83.8 1.7 %copy-done.2 = bf16[1,256,3584]{2,1,0:T(8,128)(2,1)S(1)} copy-done((bf16[1,256,3584]{2,1,0:T(8,128)(2,1)S(1)}, bf16[1,256,3584]{2,1,0:T(8,128)(2,1)}, u32[]{:S(2)}) %copy-start.2) | copy-done | bytes 1835032
  85.5 1.1 fusion.14
  87.1 1.4 multiply_convert_fusion.3
  88.5 1.1 fusion.16
  89.7 1.1 convolution_add_fusion
  91.4 3.7 %collective-permute-done.7 = bf16[256,3712]{1,0:T(8,128)(2,1)S(1)} collective-permute-done((bf16[256,3712]{1,0:T(8,128)(2,1)S(1)}, bf16[256,3712]{1,0:T(8,128)(2,1)S(1)}, u32[]{:S(2)}, u32[]{:S(2)}) %collective-permute-start.7) | collective-permute-done | bytes 1900576 | tf_op jit(solution)/shard_map/ppermute | solution.py:23
  95.8 3.2 %collective-permute-start.8 = (bf16[32,3712]{1,0:T(8,128)(2,1)S(1)}, bf16[32,3712]{1,0:T(8,128)(2,1)S(1)}, u32[]{:S(2)}, u32[]{:S(2)}) collective-permute-start(bf16[32,3712]{1,0:T(8,128)(2,1)S(1)} %get-tuple-element.17), channel_id=1, source_target_pairs={{0,32},{32,64},{64,96},{96,0},{1,33},{33,65},{65,97},{97,1},{2,34}... | collective-permute-start | bytes 712712 | tf_op jit(solution)/shard_map/ppermute | solution.py:19
  99.0 5.8 %collective-permute-done.10 = bf16[32,3712]{1,0:T(8,128)(2,1)S(1)} collective-permute-done((bf16[32,3712]{1,0:T(8,128)(2,1)S(1)}, bf16[32,3712]{1,0:T(8,128)(2,1)S(1)}, u32[]{:S(2)}, u32[]{:S(2)}) %collective-permute-start.10) | collective-permute-done | bytes 237600 | tf_op jit(solution)/shard_map/ppermute | solution.py:19
  104.9 3.0 %collective-permute-start.9 = (bf16[64,3712]{1,0:T(8,128)(2,1)S(1)}, bf16[64,3712]{1,0:T(8,128)(2,1)S(1)}, u32[]{:S(2)}, u32[]{:S(2)}) collective-permute-start(bf16[64,3712]{1,0:T(8,128)(2,1)S(1)} %pad_maximum_fusion.4), channel_id=1, source_target_pairs={{0,32},{32,64},{64,96},{96,0},{1,33},{33,65},{65,97},{97,1},{2,34}... | collective-permute-start | bytes 1425416 | tf_op jit(solution)/shard_map/ppermute | solution.py:19
  108.1 9.1 %collective-permute-done.9 = bf16[64,3712]{1,0:T(8,128)(2,1)S(1)} collective-permute-done((bf16[64,3712]{1,0:T(8,128)(2,1)S(1)}, bf16[64,3712]{1,0:T(8,128)(2,1)S(1)}, u32[]{:S(2)}, u32[]{:S(2)}) %collective-permute-start.9) | collective-permute-done | bytes 475168 | tf_op jit(solution)/shard_map/ppermute | solution.py:19
  117.2 3.5 %collective-permute-done.11 = bf16[64,3712]{1,0:T(8,128)(2,1)S(1)} collective-permute-done((bf16[64,3712]{1,0:T(8,128)(2,1)S(1)}, bf16[64,3712]{1,0:T(8,128)(2,1)S(1)}, u32[]{:S(2)}, u32[]{:S(2)}) %collective-permute-start.11) | collective-permute-done | bytes 475168 | tf_op jit(solution)/shard_map/ppermute | solution.py:19
  120.9 0.9 reshape.90
  121.9 8.8 %all-to-all-start.1 = ((bf16[32,2,3712]{2,1,0:T(2,128)(2,1)}), bf16[32,2,3712]{2,1,0:T(2,128)(2,1)S(1)}, u32[]{:S(2)}, u32[]{:S(2)}) async-start(bf16[32,2,3712]{2,1,0:T(2,128)(2,1)} %reshape.90), calls=%async_computation.1 | async-start | bytes 950272 | tf_op jit(solution)/shard_map/all_to_all | solution.py:133
  130.7 4.4 %fusion.1 = bf16[1,256,3584]{2,1,0:T(8,128)(2,1)} fusion(bf16[512,256]{0,1:T(8,128)(2,1)S(1)} %get-tuple-element.23, bf16[512,7296]{1,0:T(8,128)(2,1)} %copy-done.4), kind=kOutput, calls=%fused_computation.8 | convolution fusion | flops 940441600 | bytes 5767168 | tf_op jit(solution)/shard_map/dot_general | solution.py:113
  135.1 4.4 %fusion = bf16[1,256,3584]{2,1,0:T(8,128)(2,1)} fusion(bf16[512,256]{0,1:T(8,128)(2,1)S(1)} %get-tuple-element.21, bf16[512,7296]{1,0:T(8,128)(2,1)} %copy-done.4), kind=kOutput, calls=%fused_computation.7 | convolution fusion | flops 940441600 | bytes 5767168 | tf_op jit(solution)/shard_map/dot_general | solution.py:112
  139.6 4.7 %fusion.2 = bf16[1,256,3584]{2,1,0:T(8,128)(2,1)} fusion(f32[512]{0:T(512)S(1)} %convert_reduce_fusion, bf16[512,7296]{1,0:T(8,128)(2,1)} %copy-done.4, f32[512,256]{0,1:T(8,128)S(1)} %copy-done.7, f32[512,256]{0,1:T(8,128)S(1)} %fusion.12), kind=kOutput, calls=%fused_computation.9 | convolution fusion | flops 946733056 | bytes 6555648 | tf_op jit(solution)/shard_map/dot_general | solution.py:106
  144.3 1.6 %all-to-all-done.1 = bf16[32,2,3712]{2,1,0:T(2,128)(2,1)S(1)} async-done(((bf16[32,2,3712]{2,1,0:T(2,128)(2,1)}), bf16[32,2,3712]{2,1,0:T(2,128)(2,1)S(1)}, u32[]{:S(2)}, u32[]{:S(2)}) %all-to-all-start.1) | async-done | bytes 475168 | tf_op jit(solution)/shard_map/all_to_all | solution.py:133
  146.2 1.4 convolution_convert_fusion.3
  (61 shorter events, 7.1 us)
Async XLA Ops:
  0.6 82.0 %copy-start = (bf16[1,256,3584]{2,1,0:T(8,128)(2,1)S(1)}, bf16[1,256,3584]{2,1,0:T(8,128)(2,1)}, u32[]{:S(2)}) copy-start(bf16[1,256,3584]{2,1,0:T(8,128)(2,1)} %param.13) | copy-start | bytes 5505028
  3.9 1.8 %copy-start.3 = (bf16[128,3584]{1,0:T(8,128)(2,1)S(1)}, bf16[128,3584]{1,0:T(8,128)(2,1)}, u32[]{:S(2)}) copy-start(bf16[128,3584]{1,0:T(8,128)(2,1)} %param.10) | copy-start | bytes 2752516
  47.7 20.8 %collective-permute-start = (bf16[64,7296]{1,0:T(8,128)(2,1)S(1)}, bf16[64,7296]{1,0:T(8,128)(2,1)S(1)}, u32[]{:S(2)}, u32[]{:S(2)}) collective-permute-start(bf16[64,7296]{1,0:T(8,128)(2,1)S(1)} %reshape.89), channel_id=1, source_target_pairs={{0,32},{32,64},{64,96},{96,0},{1,33},{33,65},{65,97},{97,1},{2,34}... | collective-permute-start | bytes 2801672 | tf_op jit(solution)/shard_map/ppermute | solution.py:19
  48.0 21.4 %collective-permute-start.1 = (bf16[64,7296]{1,0:T(8,128)(2,1)S(1)}, bf16[64,7296]{1,0:T(8,128)(2,1)S(1)}, u32[]{:S(2)}, u32[]{:S(2)}) collective-permute-start(bf16[64,7296]{1,0:T(8,128)(2,1)S(1)} %reshape.89), channel_id=1, source_target_pairs={{0,96},{32,0},{64,32},{96,64},{1,97},{33,1},{65,33},{97,65},{2,98}... | collective-permute-start | bytes 2801672 | tf_op jit(solution)/shard_map/ppermute | solution.py:19
  49.8 30.2 %collective-permute-start.4 = (bf16[64,7296]{1,0:T(8,128)(2,1)S(1)}, bf16[64,7296]{1,0:T(8,128)(2,1)S(1)}, u32[]{:S(2)}, u32[]{:S(2)}) collective-permute-start(bf16[64,7296]{1,0:T(8,128)(2,1)S(1)} %reshape.89), channel_id=1, source_target_pairs={{0,16},{16,0},{1,17},{17,1},{2,18},{18,2},{3,19},{19,3},{4,20},{20... | collective-permute-start | bytes 2801672 | tf_op jit(solution)/shard_map/ppermute | solution.py:23
  68.6 9.2 %collective-permute-start.2 = (bf16[32,7296]{1,0:T(8,128)(2,1)S(1)}, bf16[32,7296]{1,0:T(8,128)(2,1)S(1)}, u32[]{:S(2)}, u32[]{:S(2)}) collective-permute-start(bf16[32,7296]{1,0:T(8,128)(2,1)S(1)} %slice.141), channel_id=1, source_target_pairs={{0,32},{32,64},{64,96},{96,0},{1,33},{33,65},{65,97},{97,1},{2,34}... | collective-permute-start | bytes 1400840 | tf_op jit(solution)/shard_map/ppermute | solution.py:19
  69.4 10.1 %collective-permute-start.3 = (bf16[32,7296]{1,0:T(8,128)(2,1)S(1)}, bf16[32,7296]{1,0:T(8,128)(2,1)S(1)}, u32[]{:S(2)}, u32[]{:S(2)}) collective-permute-start(bf16[32,7296]{1,0:T(8,128)(2,1)S(1)} %slice.142), channel_id=1, source_target_pairs={{0,96},{32,0},{64,32},{96,64},{1,97},{33,1},{65,33},{97,65},{2,98}... | collective-permute-start | bytes 1400840 | tf_op jit(solution)/shard_map/ppermute | solution.py:19
  70.9 9.2 %collective-permute-start.5 = (bf16[128,7296]{1,0:T(8,128)(2,1)S(1)}, bf16[128,7296]{1,0:T(8,128)(2,1)S(1)}, u32[]{:S(2)}, u32[]{:S(2)}) collective-permute-start(bf16[128,7296]{1,0:T(8,128)(2,1)S(1)} %pad_maximum_fusion.1), channel_id=1, source_target_pairs={{0,16},{16,0},{1,17},{17,1},{2,18},{18,2},{3,19},{19,3},{4,20},{20... | collective-permute-start | bytes 5603336 | tf_op jit(solution)/shard_map/ppermute | solution.py:23
  79.6 2.8 %collective-permute-start.6 = (bf16[64,7296]{1,0:T(8,128)(2,1)S(1)}, bf16[64,7296]{1,0:T(8,128)(2,1)S(1)}, u32[]{:S(2)}, u32[]{:S(2)}) collective-permute-start(bf16[64,7296]{1,0:T(8,128)(2,1)S(1)} %pad_maximum_fusion.3), channel_id=1, source_target_pairs={{0,16},{16,0},{1,17},{17,1},{2,18},{18,2},{3,19},{19,3},{4,20},{20... | collective-permute-start | bytes 2801672 | tf_op jit(solution)/shard_map/ppermute | solution.py:23
  82.5 4.2 %copy-start.4 = (bf16[512,7296]{1,0:T(8,128)(2,1)}, bf16[512,7296]{1,0:T(8,128)(2,1)S(1)}, u32[]{:S(2)}) copy-start(bf16[512,7296]{1,0:T(8,128)(2,1)S(1)} %constant_dynamic-update-slice_fusion) | copy-start | bytes 22413316
  82.6 2.9 %copy-start.2 = (bf16[1,256,3584]{2,1,0:T(8,128)(2,1)S(1)}, bf16[1,256,3584]{2,1,0:T(8,128)(2,1)}, u32[]{:S(2)}) copy-start(bf16[1,256,3584]{2,1,0:T(8,128)(2,1)} %param.14) | copy-start | bytes 5505028
  85.5 1.6 %copy-start.5 = (bf16[1,256,3584]{2,1,0:T(8,128)(2,1)S(1)}, bf16[1,256,3584]{2,1,0:T(8,128)(2,1)}, u32[]{:S(2)}) copy-start(bf16[1,256,3584]{2,1,0:T(8,128)(2,1)} %param.15) | copy-start | bytes 5505028
  87.1 1.4 copy-start.6
  91.2 4.0 %collective-permute-start.7 = (bf16[256,3712]{1,0:T(8,128)(2,1)S(1)}, bf16[256,3712]{1,0:T(8,128)(2,1)S(1)}, u32[]{:S(2)}, u32[]{:S(2)}) collective-permute-start(bf16[256,3712]{1,0:T(8,128)(2,1)S(1)} %fusion.5), channel_id=1, source_target_pairs={{0,16},{16,0},{1,17},{17,1},{2,18},{18,2},{3,19},{19,3},{4,20},{20... | collective-permute-start | bytes 5701640 | tf_op jit(solution)/shard_map/ppermute | solution.py:23
  95.7 9.1 %collective-permute-start.10 = (bf16[32,3712]{1,0:T(8,128)(2,1)S(1)}, bf16[32,3712]{1,0:T(8,128)(2,1)S(1)}, u32[]{:S(2)}, u32[]{:S(2)}) collective-permute-start(bf16[32,3712]{1,0:T(8,128)(2,1)S(1)} %get-tuple-element.18), channel_id=1, source_target_pairs={{0,96},{32,0},{64,32},{96,64},{1,97},{33,1},{65,33},{97,65},{2,98}... | collective-permute-start | bytes 712712 | tf_op jit(solution)/shard_map/ppermute | solution.py:19
  95.8 9.0 %collective-permute-start.8 = (bf16[32,3712]{1,0:T(8,128)(2,1)S(1)}, bf16[32,3712]{1,0:T(8,128)(2,1)S(1)}, u32[]{:S(2)}, u32[]{:S(2)}) collective-permute-start(bf16[32,3712]{1,0:T(8,128)(2,1)S(1)} %get-tuple-element.17), channel_id=1, source_target_pairs={{0,32},{32,64},{64,96},{96,0},{1,33},{33,65},{65,97},{97,1},{2,34}... | collective-permute-start | bytes 712712 | tf_op jit(solution)/shard_map/ppermute | solution.py:19
  104.9 12.3 %collective-permute-start.9 = (bf16[64,3712]{1,0:T(8,128)(2,1)S(1)}, bf16[64,3712]{1,0:T(8,128)(2,1)S(1)}, u32[]{:S(2)}, u32[]{:S(2)}) collective-permute-start(bf16[64,3712]{1,0:T(8,128)(2,1)S(1)} %pad_maximum_fusion.4), channel_id=1, source_target_pairs={{0,32},{32,64},{64,96},{96,0},{1,33},{33,65},{65,97},{97,1},{2,34}... | collective-permute-start | bytes 1425416 | tf_op jit(solution)/shard_map/ppermute | solution.py:19
  108.0 12.8 %collective-permute-start.11 = (bf16[64,3712]{1,0:T(8,128)(2,1)S(1)}, bf16[64,3712]{1,0:T(8,128)(2,1)S(1)}, u32[]{:S(2)}, u32[]{:S(2)}) collective-permute-start(bf16[64,3712]{1,0:T(8,128)(2,1)S(1)} %pad_maximum_fusion.5), channel_id=1, source_target_pairs={{0,96},{32,0},{64,32},{96,64},{1,97},{33,1},{65,33},{97,65},{2,98}... | collective-permute-start | bytes 1425416 | tf_op jit(solution)/shard_map/ppermute | solution.py:19
  121.9 24.0 %all-to-all-start.1 = ((bf16[32,2,3712]{2,1,0:T(2,128)(2,1)}), bf16[32,2,3712]{2,1,0:T(2,128)(2,1)S(1)}, u32[]{:S(2)}, u32[]{:S(2)}) async-start(bf16[32,2,3712]{2,1,0:T(2,128)(2,1)} %reshape.90), calls=%async_computation.1 | async-start | bytes 950272 | tf_op jit(solution)/shard_map/all_to_all | solution.py:133
  135.1 4.4 %copy-start.7 = (f32[512,256]{0,1:T(8,128)S(1)}, f32[512,256]{0,1:T(8,128)}, u32[]{:S(2)}) copy-start(f32[512,256]{0,1:T(8,128)} %copy-done.6) | copy-start | bytes 1572868
  139.6 8.7 %copy-start.1 = (bf16[1,256,3584]{2,1,0:T(8,128)(2,1)S(1)}, bf16[1,256,3584]{2,1,0:T(8,128)(2,1)}, u32[]{:S(2)}) copy-start(bf16[1,256,3584]{2,1,0:T(8,128)(2,1)} %param.13) | copy-start | bytes 5505028

commit v2 on v1

v2 whole, which is shorter than its diff:
```python
import functools

import jax
import jax.numpy as jnp
from jax import lax
from jax.experimental import pallas as pl
from jax.experimental.pallas import tpu as pltpu
from jax.sharding import Mesh, PartitionSpec as P

EXP_DEV = 16
CAP = 2
SCALE_BLOCK = 128
LANES = 128
CHUNK = 512

rows_pair = (((0,), (0,)), ((), ()))
last_pair = (((1,), (1,)), ((), ()))

COLUMN = ("zlo", "zhi", "x")
MIB = 1 << 20
F32 = jnp.float32
BF16 = jnp.bfloat16


def along_y(value, step):
    count = lax.axis_size("y")
    return lax.ppermute(value, "y", [(i, (i + step) % count) for i in range(count)])


def swap_core(value):
    return lax.ppermute(value, "core", [(0, 1), (1, 0)])


def in_hbm(value):
    return pltpu.with_memory_space_constraint(value, pltpu.HBM)


def call(kernel, outs, scratch, vmem, cost, *args, space=pltpu.VMEM, out_space=None):
    flops, moved = cost
    if out_space is None:
        out_shape = [jax.ShapeDtypeStruct(s, t) for s, t in outs]
    else:
        out_shape = [out_space(s, t) for s, t in outs]
    return pl.pallas_call(
        kernel,
        out_shape=out_shape,
        in_specs=[pl.BlockSpec(memory_space=space)] * len(args),
        out_specs=[pl.BlockSpec(memory_space=pltpu.VMEM)] * len(outs),
        scratch_shapes=scratch,
        compiler_params=pltpu.CompilerParams(vmem_limit_bytes=vmem * MIB),
        cost_estimate=pl.CostEstimate(
            flops=flops, bytes_accessed=moved, transcendentals=0
        ),
    )(*args)


def dot(left, right, dims=(((1,), (0,)), ((), ()))):
    return lax.dot_general(left, right, dims, preferred_element_type=F32)


def slot_targets(slots):
    slot = lax.broadcasted_iota(jnp.int32, (slots, 1), 0)
    group = slot // CAP
    half = slots // CAP // 2
    target = (group % half) * EXP_DEV + (group // half) * (EXP_DEV // 2)
    return target, slot % CAP


def fetch_all(sources, local, sems):
    copies = [
        pltpu.make_async_copy(source, target, sems.at[k])
        for k, (source, target) in enumerate(zip(sources, local, strict=True))
    ]
    for copy in copies:
        copy.start()
    return copies


def send_kernel(*refs):
    send_ref, kept_ref, tail_ref = refs[4:7]
    ids_ref, combine_ref, scale_ref, quant_ref = local = refs[7:11]
    copies = fetch_all(refs[:4], local, refs[11])
    top, tokens = ids_ref.shape
    slots = kept_ref.shape[0]
    width = quant_ref.shape[1]
    target, rank = slot_targets(slots)
    row = lax.broadcasted_iota(jnp.int32, (tokens, tokens), 0)
    col = lax.broadcasted_iota(jnp.int32, (tokens, tokens), 1)
    earlier = (row < col).astype(F32).astype(BF16)
    hit = jnp.zeros((slots, tokens), F32)
    weight = jnp.zeros((slots, tokens), F32)
    copies[0].wait()
    copies[1].wait()
    for k in range(top):
        one = ids_ref[k : k + 1, :] == target
        hit = hit + one.astype(F32)
        weight = weight + jnp.where(one, combine_ref[k : k + 1, :].astype(F32), 0.0)
    place = dot(hit.astype(BF16), earlier)
    kept = jnp.where(place == rank.astype(F32), hit, 0.0)
    kept_b = kept.astype(BF16)
    kept_ref[...] = kept_b
    picked = jnp.sum(kept * weight, axis=1, keepdims=True)
    tail_ref[...] = jnp.broadcast_to(picked, tail_ref.shape).astype(BF16)
    copies[2].wait()
    scales = dot(kept_b, scale_ref[...], last_pair)
    copies[3].wait()
    for c in range(0, width, CHUNK):
        rows = dot(kept_b, quant_ref[:, c : c + CHUNK])
        for i in range(0, CHUNK, SCALE_BLOCK):
            b = (c + i) // SCALE_BLOCK
            send_ref[:, c + i : c + i + SCALE_BLOCK] = (
                rows[:, i : i + SCALE_BLOCK] * scales[:, b : b + 1]
            ).astype(BF16)


def pick_kernel(kept_ref, dy_ref, tail_ref, out_ref):
    width = dy_ref.shape[1]
    for c in range(0, width, CHUNK):
        at = pl.ds(c, CHUNK)
        out_ref[:, at] = dot(kept_ref[...], dy_ref[:, at]).astype(BF16)
    out_ref[:, width:] = tail_ref[...]


def home_kernel(home_ref, kept_ref, ids_ref, in_ref, combine_ref):
    width = in_ref.shape[1]
    top, tokens = ids_ref.shape
    slots = kept_ref.shape[0]
    kept = kept_ref[...]
    for c in range(0, width, CHUNK):
        at = pl.ds(c, CHUNK)
        in_ref[:, at] = dot(kept, home_ref[:, at], rows_pair).astype(BF16)
    target, _ = slot_targets(slots)
    value = kept.astype(F32) * home_ref[:, width : width + 1].astype(F32)
    for k in range(top):
        mine = jnp.where(ids_ref[k : k + 1, :] == target, value, 0.0)
        combine_ref[k : k + 1, :] = jnp.sum(mine, axis=0, keepdims=True).astype(BF16)


def body(quant_rows, row_scales, out_grad, combine, expert_ids, gate_w, up_w, down_w):
    top_count = expert_ids.shape[1]
    width = quant_rows.shape[1]
    groups = lax.axis_size("zlo") * lax.axis_size("zhi") * lax.axis_size("x")
    tokens = quant_rows.shape[0]
    units = gate_w.shape[1]
    slots = groups * CAP
    wide = width + LANES
    sources = [in_hbm(v) for v in (expert_ids.T, combine.T, row_scales.T, quant_rows)]
    send_x, kept, tail = call(
        send_kernel,
        [((slots, width), BF16), ((slots, tokens), BF16), ((slots, LANES), BF16)],
        [pltpu.VMEM(v.shape, v.dtype) for v in sources]
        + [pltpu.SemaphoreType.DMA((len(sources),))],
        8,
        (2 * tokens * slots * width, MIB),
        *sources,
        space=pltpu.HBM,
    )
    (send_d,) = call(
        pick_kernel,
        [((slots, wide), BF16)],
        [],
        8,
        (2 * tokens * slots * width, 2 * MIB),
        kept,
        out_grad,
        tail,
    )
    half = slots // 2

    def spread(send):
        wide = send.shape[1]
        own = lax.all_to_all(
            send.reshape(groups, CAP, wide),
            COLUMN,
            split_axis=0,
            concat_axis=0,
            tiled=True,
        ).reshape(slots, wide)
        below = along_y(own, 1)
        above = along_y(own, -1)
        far_low = along_y(below[:half], 1)
        far_high = along_y(above[half:], -1)
        near = jnp.concatenate([own, below, above], axis=0)
        near = jnp.concatenate([near, swap_core(near)], axis=0)
        return near, (far_low, far_high)

    gate_rows = gate_w[0]
    up_rows = up_w[0]
    down_rows = down_w[0]

    def work(x, dy_wide):
        dy = dy_wide[:, :width]
        weight = dy_wide[:, width : width + 1].astype(jnp.float32)
        h_gate = lax.dot_general(
            x, gate_rows, last_pair, preferred_element_type=jnp.float32
        )
        h_up = lax.dot_general(x, up_rows, last_pair, preferred_element_type=jnp.float32)
        sig = jax.nn.sigmoid(h_gate)
        act = h_gate * sig * h_up
        back = lax.dot_general(
            dy, down_rows, last_pair, preferred_element_type=jnp.float32
        )
        gate_part = jnp.sum(act * back, axis=1)
        scaled = (weight * dy.astype(jnp.float32)).astype(jnp.bfloat16)
        d_act = weight * back
        dh_up = (d_act * h_gate * sig).astype(jnp.bfloat16)
        dh_gate = (d_act * h_up * sig * (1.0 + h_gate * (1.0 - sig))).astype(
            jnp.bfloat16
        )
        part = jnp.dot(dh_gate, gate_rows, preferred_element_type=jnp.float32)
        part = part + jnp.dot(dh_up, up_rows, preferred_element_type=jnp.float32)
        part = jnp.concatenate(
            [part, jnp.broadcast_to(gate_part[:, None], (part.shape[0], LANES))], axis=1
        )
        count = part.shape[0] // 2
        mine = part[:count] + swap_core(part[count:].astype(jnp.bfloat16)).astype(
            jnp.float32
        )
        return mine, act.astype(jnp.bfloat16), scaled, dh_gate, dh_up

    near_x, far_x = spread(send_x)
    near_d, far_d = spread(send_d)
    near_sum, near_act, near_scaled, near_gate, near_up = work(near_x, near_d)
    far_x, far_d, _ = lax.optimization_barrier((far_x, far_d, (near_act, near_gate, near_up)))
    far_x, far_d = (jnp.concatenate(v, axis=0) for v in (far_x, far_d))
    far_x, far_d = (jnp.concatenate([v, swap_core(v)], axis=0) for v in (far_x, far_d))
    far_sum, far_act, far_scaled, far_gate, far_up = work(far_x, far_d)

    def weight_grad(a_near, a_far, b_near, b_far):
        return lax.dot_general(
            jnp.concatenate([a_near, a_far], axis=0),
            jnp.concatenate([b_near, b_far], axis=0),
            rows_pair,
            preferred_element_type=jnp.float32,
        )

    grad_gate = weight_grad(near_gate, far_gate, near_x, far_x)
    grad_up = weight_grad(near_up, far_up, near_x, far_x)
    grad_down = weight_grad(near_act, far_act, near_scaled, far_scaled)

    def send_y(value, step):
        return along_y(value.astype(jnp.bfloat16), step).astype(jnp.float32)

    s_own, s_below, s_above = (near_sum[k * slots : (k + 1) * slots] for k in range(3))
    above_low = s_above[:half] + send_y(far_sum[:half], 1)
    below_high = s_below[half:] + send_y(far_sum[half:], -1)
    high = s_own[half:] + send_y(s_above[half:], 1)
    low = s_own[:half] + send_y(s_below[:half], -1)
    low = low + send_y(above_low, 1)
    high = high + send_y(below_high, -1)
    total = jnp.concatenate([low, high], axis=0).astype(jnp.bfloat16)
    home = lax.all_to_all(
        total.reshape(groups, CAP, -1), COLUMN, split_axis=0, concat_axis=0, tiled=True
    ).reshape(slots, -1)
    in_grad, combine_grad = call(
        home_kernel,
        [((tokens, width), BF16), ((top_count, tokens), BF16)],
        [],
        8,
        (2 * tokens * slots * width, 2 * MIB),
        home,
        kept,
        expert_ids.T,
    )
    return (
        in_grad,
        combine_grad.T,
        grad_gate.astype(jnp.bfloat16)[None],
        grad_up.astype(jnp.bfloat16)[None],
        grad_down.astype(jnp.bfloat16)[None],
    )


def solution(mesh):
    fine = Mesh(
        mesh.devices.reshape(2, 4, 2, 4, 4), ("zlo", "y", "core", "zhi", "x")
    )
    tokens = P(("zlo", "y", "core", "zhi", "x"), None)
    hidden = P(("zhi", "x"), ("zlo", "y", "core"), None)
    return jax.shard_map(
        body,
        mesh=fine,
        in_specs=(tokens,) * 5 + (hidden,) * 3,
        out_specs=(tokens,) * 2 + (hidden,) * 3,
        check_vma=False,
    )
```

time: 149 us -> 133 us (0.89)
  blocking collectives: 37.8 us -> 0 us
  starting transfers between devices: 20.1 us -> 39.7 us
  matrix products: 21.9 us -> 18 us
  Pallas kernels: 0 us -> 3.42 us
  other arithmetic: 3.27 us -> 6.17 us
  waiting for transfers between devices: 52.8 us -> 50.9 us
  local copies, waits for them, and re-layouts: 11.4 us -> 13.2 us
    all_to_all x1 -> x0, blocking collectives: 37.8 us -> none  [body(): lax.all_to_all(send.reshape(groups, CAP, wide), COLUMN, split_axis=0, con...]
    ppermute x8 -> x14, waiting for transfers between devices: 45.4 us -> 16.3 us  [along_y(): lax.ppermute(value, 'y', [(i, (i + step) % count) for i in range(count)])]
    all_to_all x0 -> x2, waiting for transfers between devices: none -> 27.6 us  [spread(): lax.all_to_all(send.reshape(groups, CAP, wide), COLUMN, split_axis=0, con...]
    all_to_all x0 -> x2, starting transfers between devices: none -> 16 us  [spread(): lax.all_to_all(send.reshape(groups, CAP, wide), COLUMN, split_axis=0, con...]
    ppermute x8 -> x14, starting transfers between devices: 10.7 us -> 15.3 us  [along_y(): lax.ppermute(value, 'y', [(i, (i + step) % count) for i in range(count)])]
    ppermute x4 -> x6, waiting for transfers between devices: 5.75 us -> 1.84 us  [swap_core(): return lax.ppermute(value, 'core', [(0, 1), (1, 0)])]
    dot_general x12 -> x13, matrix products: 21.9 us -> 18 us  [the longest x3 9.16 us: weight_grad(): lax.dot_general(jnp.concatenate([a_near, a_far], axis=0), jnp.concatenate...]
    all_to_all x1, waiting for transfers between devices: 1.61 us -> 5.1 us  [body(): lax.all_to_all(total.reshape(groups, CAP, -1), COLUMN, split_axis=0, conc...]
  transfers between devices with their start and end apart: 13 -> 23, of which waited for: 9 -> 14; matrix products, arithmetic and copies ran while one was open for 10% -> 23% of each run, Pallas kernels for 0% -> 0%
where the time goes in v2:
time: 133 us
  waiting for transfers between devices  50.9 us (38%)
  starting transfers between devices  39.7 us (30%)
  matrix products  18 us (14%)
  local copies, waits for them, and re-layouts  13.2 us (10%)
  other arithmetic  6.17 us (5%)
  Pallas kernels  3.42 us (3%)
    all_to_all x2, waiting for transfers between devices, spread(): lax.all_to_all(send.reshape(groups, CAP, wide), COLUMN, split_axis=0, con...  27.6 us
    ppermute x14, waiting for transfers between devices, along_y(): lax.ppermute(value, 'y', [(i, (i + step) % count) for i in range(count)])  16.3 us
    all_to_all x2, starting transfers between devices, spread(): lax.all_to_all(send.reshape(groups, CAP, wide), COLUMN, split_axis=0, con...  16 us
    ppermute x14, starting transfers between devices, along_y(): lax.ppermute(value, 'y', [(i, (i + step) % count) for i in range(count)])  15.3 us
    dot_general x3, matrix products, weight_grad(): lax.dot_general(jnp.concatenate([a_near, a_far], axis=0), jnp.concatenate...  9.16 us
    all_to_all x1, starting transfers between devices, body(): lax.all_to_all(total.reshape(groups, CAP, -1), COLUMN, split_axis=0, conc...  6.89 us
    unnamed x35, local copies, waits for them, and re-layouts  6.26 us
    all_to_all x1, waiting for transfers between devices, body(): lax.all_to_all(total.reshape(groups, CAP, -1), COLUMN, split_axis=0, conc...  5.1 us
  transfers between devices with their start and end apart: 23, of which 14 were waited for; matrix products, arithmetic and copies ran while one was open for 23% of the time, Pallas kernels for 0%

profile of v2, /device:TPU:24, one launch (start us, length us, event | category | flops | bytes accessed | tf_op | source)
XLA Modules:
  0.0 132.5 jit_solution(15250379697499362440)
XLA Ops:
  0.7 1.8 %shard_map.119 = (bf16[64,3584]{1,0:T(8,128)(2,1)S(1)}, bf16[64,128]{1,0:T(8,128)(2,1)S(1)}, bf16[64,128]{1,0:T(8,128)(2,1)S(1)}) custom-call(s32[8,128]{1,0:T(8,128)} %bitcast.47, bf16[8,128]{1,0:T(8,128)(2,1)} %bitcast.50, bf16[28,128]{1,0:T(8,128)(2,1)} %bitcast.49, bf16[128,3584]{1,0:T(8,128)(2,1)} %refs_3_.1), custom_call_target="tpu_custom_call" | custom-call | flops 58720256 | bytes 1048576 | tf_op jit(solution)/shard_map/pallas_call | solution.py:44
  3.4 11.4 %all-to-all-start.1 = ((bf16[32,2,3584]{2,1,0:T(2,128)(2,1)}), bf16[32,2,3584]{2,1,0:T(2,128)(2,1)}, u32[]{:S(2)}, u32[]{:S(2)}) async-start(bf16[32,2,3584]{2,1,0:T(2,128)(2,1)} %reshape.32), calls=%async_computation.1 | async-start | bytes 917504 | tf_op jit(solution)/shard_map/all_to_all | solution.py:172
  16.1 15.8 %all-to-all-done.1 = bf16[32,2,3584]{2,1,0:T(2,128)(2,1)} async-done(((bf16[32,2,3584]{2,1,0:T(2,128)(2,1)}), bf16[32,2,3584]{2,1,0:T(2,128)(2,1)}, u32[]{:S(2)}, u32[]{:S(2)}) %all-to-all-start.1) | async-done | bytes 458784 | tf_op jit(solution)/shard_map/all_to_all | solution.py:172
  31.9 4.6 %all-to-all-start = ((bf16[32,2,3712]{2,1,0:T(2,128)(2,1)}), bf16[32,2,3712]{2,1,0:T(2,128)(2,1)}, u32[]{:S(2)}, u32[]{:S(2)}) async-start(bf16[32,2,3712]{2,1,0:T(2,128)(2,1)} %reshape.30), calls=%async_computation | async-start | bytes 950272 | tf_op jit(solution)/shard_map/all_to_all | solution.py:172
  36.5 1.2 reshape.33
  38.0 1.8 %collective-permute-start.4 = (bf16[64,3584]{1,0:T(8,128)(2,1)S(1)}, bf16[64,3584]{1,0:T(8,128)(2,1)S(1)}, u32[]{:S(2)}, u32[]{:S(2)}) collective-permute-start(bf16[64,3584]{1,0:T(8,128)(2,1)S(1)} %reshape.33), channel_id=1, source_target_pairs={{0,96},{32,0},{64,32},{96,64},{1,97},{33,1},{65,33},{97,65},{2,98}... | collective-permute-start | bytes 1376264 | tf_op jit(solution)/shard_map/ppermute | solution.py:27
  40.8 11.8 %all-to-all-done = bf16[32,2,3712]{2,1,0:T(2,128)(2,1)} async-done(((bf16[32,2,3712]{2,1,0:T(2,128)(2,1)}), bf16[32,2,3712]{2,1,0:T(2,128)(2,1)}, u32[]{:S(2)}, u32[]{:S(2)}) %all-to-all-start) | async-done | bytes 475168 | tf_op jit(solution)/shard_map/all_to_all | solution.py:172
  52.6 1.2 reshape.31
  54.1 1.8 %collective-permute-start.1 = (bf16[64,3712]{1,0:T(8,128)(2,1)S(1)}, bf16[64,3712]{1,0:T(8,128)(2,1)S(1)}, u32[]{:S(2)}, u32[]{:S(2)}) collective-permute-start(bf16[64,3712]{1,0:T(8,128)(2,1)S(1)} %reshape.31), channel_id=1, source_target_pairs={{0,96},{32,0},{64,32},{96,64},{1,97},{33,1},{65,33},{97,65},{2,98}... | collective-permute-start | bytes 1425416 | tf_op jit(solution)/shard_map/ppermute | solution.py:27
  58.1 1.5 %collective-permute-start.8 = (bf16[32,3584]{1,0:T(8,128)(2,1)S(1)}, bf16[32,3584]{1,0:T(8,128)(2,1)S(1)}, u32[]{:S(2)}, u32[]{:S(2)}) collective-permute-start(bf16[32,3584]{1,0:T(8,128)(2,1)S(1)} %slice.102), channel_id=1, source_target_pairs={{0,32},{32,64},{64,96},{96,0},{1,33},{33,65},{65,97},{97,1},{2,34}... | collective-permute-start | bytes 688136 | tf_op jit(solution)/shard_map/ppermute | solution.py:27
  60.3 1.9 %constant_dynamic-update-slice_fusion.19 = (bf16[512,3584]{1,0:T(8,128)(2,1)S(1)}, bf16[384,3584]{1,0:T(8,128)(2,1)}) fusion(bf16[512,3584]{1,0:T(8,128)(2,1)S(1)} %copy-done.3, bf16[64,3584]{1,0:T(8,128)(2,1)} %collective-permute-done.3, bf16[384,3584]{1,0:T(8,128)(2,1)} %get-tuple-element.46), kind=kLoop, calls=%fused_computation.101 | loop fusion | bytes 1376256
  64.3 1.7 %collective-permute-start.10 = (bf16[32,3712]{1,0:T(8,128)(2,1)S(1)}, bf16[32,3712]{1,0:T(8,128)(2,1)S(1)}, u32[]{:S(2)}, u32[]{:S(2)}) collective-permute-start(bf16[32,3712]{1,0:T(8,128)(2,1)S(1)} %slice.104), channel_id=1, source_target_pairs={{0,32},{32,64},{64,96},{96,0},{1,33},{33,65},{65,97},{97,1},{2,34}... | collective-permute-start | bytes 712712 | tf_op jit(solution)/shard_map/ppermute | solution.py:27
  70.9 1.7 %multiply_convert_fusion.3 = (bf16[384,256]{1,0:T(8,128)(2,1)S(1)}, f32[384]{0:T(512)S(1)}, bf16[384,256]{1,0:T(8,128)(2,1)S(1)}, bf16[384,256]{1,0:T(8,128)(2,1)}) fusion(f32[384,256]{1,0:T(8,128)S(1)} %fusion.23, f32[384,256]{1,0:T(8,128)S(1)} %fusion.9, f32[384]{0:T(512)S(1)} %convert_reduce_fusion, bf16[384,3584]{1,0:T(8,128)(2,1)S(1)} %get-tuple-element.32, ...), kind=kOutput, calls=%fused_computation.64 | convolution fusion | flops 706510464 | bytes 5966848 | tf_op jit(solution)/shard_map/dot_general | solution.py:194
  73.6 2.0 %collective-permute-done.11 = bf16[32,3712]{1,0:T(8,128)(2,1)S(1)} collective-permute-done((bf16[32,3712]{1,0:T(8,128)(2,1)S(1)}, bf16[32,3712]{1,0:T(8,128)(2,1)S(1)}, u32[]{:S(2)}, u32[]{:S(2)}) %collective-permute-start.11) | collective-permute-done | bytes 237600 | tf_op jit(solution)/shard_map/ppermute | solution.py:27
  80.2 1.3 multiply_reduce_fusion.1
  85.0 1.7 %collective-permute-start.18 = (bf16[32,3712]{1,0:T(8,128)(2,1)S(1)}, bf16[32,3712]{1,0:T(8,128)(2,1)S(1)}, u32[]{:S(2)}, u32[]{:S(2)}) collective-permute-start(bf16[32,3712]{1,0:T(8,128)(2,1)S(1)} %get-tuple-element.38), channel_id=1, source_target_pairs={{0,96},{32,0},{64,32},{96,64},{1,97},{33,1},{65,33},{97,65},{2,98}... | collective-permute-start | bytes 712712 | tf_op jit(solution)/shard_map/ppermute | solution.py:27
  87.0 5.5 %collective-permute-done.15 = bf16[32,3712]{1,0:T(8,128)(2,1)S(1)} collective-permute-done((bf16[32,3712]{1,0:T(8,128)(2,1)S(1)}, bf16[32,3712]{1,0:T(8,128)(2,1)S(1)}, u32[]{:S(2)}, u32[]{:S(2)}) %collective-permute-start.15) | collective-permute-done | bytes 237600 | tf_op jit(solution)/shard_map/ppermute | solution.py:27
  92.5 1.3 collective-permute-done.18
  94.2 1.8 %collective-permute-start.19 = (bf16[32,3712]{1,0:T(8,128)(2,1)S(1)}, bf16[32,3712]{1,0:T(8,128)(2,1)S(1)}, u32[]{:S(2)}, u32[]{:S(2)}) collective-permute-start(bf16[32,3712]{1,0:T(8,128)(2,1)S(1)} %get-tuple-element.28), channel_id=1, source_target_pairs={{0,96},{32,0},{64,32},{96,64},{1,97},{33,1},{65,33},{97,65},{2,98}... | collective-permute-start | bytes 712712 | tf_op jit(solution)/shard_map/ppermute | solution.py:27
  96.0 1.8 %collective-permute-start.17 = (bf16[32,3712]{1,0:T(8,128)(2,1)S(1)}, bf16[32,3712]{1,0:T(8,128)(2,1)S(1)}, u32[]{:S(2)}, u32[]{:S(2)}) collective-permute-start(bf16[32,3712]{1,0:T(8,128)(2,1)S(1)} %get-tuple-element.30), channel_id=1, source_target_pairs={{0,32},{32,64},{64,96},{96,0},{1,33},{33,65},{65,97},{97,1},{2,34}... | collective-permute-start | bytes 712712 | tf_op jit(solution)/shard_map/ppermute | solution.py:27
  98.4 2.4 %multiply_convert_fusion = bf16[384,3584]{1,0:T(8,128)(2,1)} fusion(f32[384]{0:T(512)S(1)} %convert_reduce_fusion, bf16[384,3712]{1,0:T(8,128)(2,1)S(1)} %constant_dynamic-update-slice_fusion), kind=kLoop, calls=%fused_computation.3 | loop fusion | flops 4128768 | bytes 5506560 | tf_op jit(solution)/shard_map/convert_element_type | solution.py:204
  100.7 2.0 %collective-permute-done.16 = bf16[32,3712]{1,0:T(8,128)(2,1)S(1)} collective-permute-done((bf16[32,3712]{1,0:T(8,128)(2,1)S(1)}, bf16[32,3712]{1,0:T(8,128)(2,1)S(1)}, u32[]{:S(2)}, u32[]{:S(2)}) %collective-permute-start.16) | collective-permute-done | bytes 237600 | tf_op jit(solution)/shard_map/ppermute | solution.py:27
  102.7 1.5 %collective-permute-done.19 = bf16[32,3712]{1,0:T(8,128)(2,1)S(1)} collective-permute-done((bf16[32,3712]{1,0:T(8,128)(2,1)S(1)}, bf16[32,3712]{1,0:T(8,128)(2,1)S(1)}, u32[]{:S(2)}, u32[]{:S(2)}) %collective-permute-start.19) | collective-permute-done | bytes 237600 | tf_op jit(solution)/shard_map/ppermute | solution.py:27
  104.1 1.6 %collective-permute-done.17 = bf16[32,3712]{1,0:T(8,128)(2,1)S(1)} collective-permute-done((bf16[32,3712]{1,0:T(8,128)(2,1)S(1)}, bf16[32,3712]{1,0:T(8,128)(2,1)S(1)}, u32[]{:S(2)}, u32[]{:S(2)}) %collective-permute-start.17) | collective-permute-done | bytes 237600 | tf_op jit(solution)/shard_map/ppermute | solution.py:27
  105.8 1.4 %collective-permute-done.7 = bf16[32,3712]{1,0:T(8,128)(2,1)S(1)} collective-permute-done((bf16[32,3712]{1,0:T(8,128)(2,1)S(1)}, bf16[32,3712]{1,0:T(8,128)(2,1)S(1)}, u32[]{:S(2)}, u32[]{:S(2)}) %collective-permute-start.7) | collective-permute-done | bytes 237600 | tf_op jit(solution)/shard_map/ppermute | solution.py:27
  108.4 6.9 %all-to-all-start.2 = ((bf16[32,2,3712]{2,1,0:T(2,128)(2,1)}), bf16[32,2,3712]{2,1,0:T(2,128)(2,1)S(1)}, u32[]{:S(2)}, u32[]{:S(2)}) async-start(bf16[32,2,3712]{2,1,0:T(2,128)(2,1)} %convert_element_type.97), calls=%async_computation.2 | async-start | bytes 950272 | tf_op jit(solution)/shard_map/all_to_all | solution.py:252
  115.3 1.4 %multiply_convert_fusion.1 = bf16[128,3584]{1,0:T(8,128)(2,1)S(1)} fusion(f32[128]{0:T(128)S(1)} %convert_reduce_fusion.1, bf16[128,3712]{1,0:T(8,128)(2,1)} %copy-done.7), kind=kLoop, calls=%fused_computation.39 | loop fusion | flops 1376256 | bytes 1835520 | tf_op jit(solution)/shard_map/convert_element_type | solution.py:204
  116.7 4.4 %fusion.2 = bf16[1,256,3584]{2,1,0:T(8,128)(2,1)} fusion(bf16[128,3584]{1,0:T(8,128)(2,1)S(1)} %multiply_convert_fusion.1, bf16[384,3584]{1,0:T(8,128)(2,1)} %multiply_convert_fusion, bf16[128,256]{1,0:T(8,128)(2,1)} %get-tuple-element.50, bf16[384,256]{1,0:T(8,128)(2,1)} %get-tuple-element.36), kind=kOutput, calls=%fused_computation.10 | convolution fusion | flops 948305920 | bytes 5767168 | tf_op jit(solution)/shard_map/dot_general | solution.py:230
  121.2 2.4 %fusion.1 = bf16[1,256,3584]{2,1,0:T(8,128)(2,1)} fusion(bf16[512,3584]{1,0:T(8,128)(2,1)S(1)} %copy-done.5, bf16[128,256]{1,0:T(8,128)(2,1)S(1)} %copy-done.9, bf16[384,256]{1,0:T(8,128)(2,1)S(1)} %get-tuple-element.35), kind=kOutput, calls=%fused_computation.9 | convolution fusion | flops 940965888 | bytes 5767168 | tf_op jit(solution)/shard_map/dot_general | solution.py:230
  123.5 2.4 %fusion = bf16[1,256,3584]{2,1,0:T(8,128)(2,1)} fusion(bf16[512,3584]{1,0:T(8,128)(2,1)S(1)} %copy-done.5, bf16[128,256]{1,0:T(8,128)(2,1)S(1)} %get-tuple-element.48, bf16[384,256]{1,0:T(8,128)(2,1)S(1)} %get-tuple-element.33), kind=kOutput, calls=%fused_computation.8 | convolution fusion | flops 940965888 | bytes 5767168 | tf_op jit(solution)/shard_map/dot_general | solution.py:230
  125.9 5.1 %all-to-all-done.2 = bf16[32,2,3712]{2,1,0:T(2,128)(2,1)S(1)} async-done(((bf16[32,2,3712]{2,1,0:T(2,128)(2,1)}), bf16[32,2,3712]{2,1,0:T(2,128)(2,1)S(1)}, u32[]{:S(2)}, u32[]{:S(2)}) %all-to-all-start.2) | async-done | bytes 475168 | tf_op jit(solution)/shard_map/all_to_all | solution.py:252
  131.2 1.4 %shard_map.121 = (bf16[128,3584]{1,0:T(8,128)(2,1)}, bf16[8,128]{1,0:T(8,128)(2,1)}) custom-call(bf16[64,3712]{1,0:T(8,128)(2,1)S(1)} %reshape.34.home_ref, bf16[64,128]{1,0:T(8,128)(2,1)S(1)} %get-tuple-element.14.kept_ref, s32[8,128]{1,0:T(8,128)S(1)} %bitcast.48), custom_call_target="tpu_custom_call" | custom-call | flops 58720256 | bytes 2097152 | tf_op jit(solution)/shard_map/pallas_call | solution.py:44
  (97 shorter events, 25.1 us)
Async XLA Ops:
  0.6 70.3 %copy-start = (bf16[1,256,3584]{2,1,0:T(8,128)(2,1)S(1)}, bf16[1,256,3584]{2,1,0:T(8,128)(2,1)}, u32[]{:S(2)}) copy-start(bf16[1,256,3584]{2,1,0:T(8,128)(2,1)} %param.13) | copy-start | bytes 5505028
  0.6 14.2 %copy-start.1 = (bf16[128,3584]{1,0:T(8,128)(2,1)S(1)}, bf16[128,3584]{1,0:T(8,128)(2,1)}, u32[]{:S(2)}) copy-start(bf16[128,3584]{1,0:T(8,128)(2,1)} %dy_ref.1) | copy-start | bytes 2752516
  3.4 28.5 %all-to-all-start.1 = ((bf16[32,2,3584]{2,1,0:T(2,128)(2,1)}), bf16[32,2,3584]{2,1,0:T(2,128)(2,1)}, u32[]{:S(2)}, u32[]{:S(2)}) async-start(bf16[32,2,3584]{2,1,0:T(2,128)(2,1)} %reshape.32), calls=%async_computation.1 | async-start | bytes 917504 | tf_op jit(solution)/shard_map/all_to_all | solution.py:172
  31.9 20.7 %all-to-all-start = ((bf16[32,2,3712]{2,1,0:T(2,128)(2,1)}), bf16[32,2,3712]{2,1,0:T(2,128)(2,1)}, u32[]{:S(2)}, u32[]{:S(2)}) async-start(bf16[32,2,3712]{2,1,0:T(2,128)(2,1)} %reshape.30), calls=%async_computation | async-start | bytes 950272 | tf_op jit(solution)/shard_map/all_to_all | solution.py:172
  37.7 18.2 %collective-permute-start.3 = (bf16[64,3584]{1,0:T(8,128)(2,1)S(1)}, bf16[64,3584]{1,0:T(8,128)(2,1)}, u32[]{:S(2)}, u32[]{:S(2)}) collective-permute-start(bf16[64,3584]{1,0:T(8,128)(2,1)S(1)} %reshape.33), channel_id=1, source_target_pairs={{0,32},{32,64},{64,96},{96,0},{1,33},{33,65},{65,97},{97,1},{2,34}... | collective-permute-start | bytes 1376264 | tf_op jit(solution)/shard_map/ppermute | solution.py:27
  38.0 17.9 %collective-permute-start.4 = (bf16[64,3584]{1,0:T(8,128)(2,1)S(1)}, bf16[64,3584]{1,0:T(8,128)(2,1)S(1)}, u32[]{:S(2)}, u32[]{:S(2)}) collective-permute-start(bf16[64,3584]{1,0:T(8,128)(2,1)S(1)} %reshape.33), channel_id=1, source_target_pairs={{0,96},{32,0},{64,32},{96,64},{1,97},{33,1},{65,33},{97,65},{2,98}... | collective-permute-start | bytes 1376264 | tf_op jit(solution)/shard_map/ppermute | solution.py:27
  53.8 6.5 %copy-start.3 = (bf16[512,3584]{1,0:T(8,128)(2,1)S(1)}, bf16[512,3584]{1,0:T(8,128)(2,1)}, u32[]{:S(2)}) copy-start(bf16[512,3584]{1,0:T(8,128)(2,1)} %get-tuple-element.45) | copy-start | bytes 11010052
  53.8 9.9 %collective-permute-start = (bf16[64,3712]{1,0:T(8,128)(2,1)S(1)}, bf16[64,3712]{1,0:T(8,128)(2,1)S(1)}, u32[]{:S(2)}, u32[]{:S(2)}) collective-permute-start(bf16[64,3712]{1,0:T(8,128)(2,1)S(1)} %reshape.31), channel_id=1, source_target_pairs={{0,32},{32,64},{64,96},{96,0},{1,33},{33,65},{65,97},{97,1},{2,34}... | collective-permute-start | bytes 1425416 | tf_op jit(solution)/shard_map/ppermute | solution.py:27
  54.1 10.0 %collective-permute-start.1 = (bf16[64,3712]{1,0:T(8,128)(2,1)S(1)}, bf16[64,3712]{1,0:T(8,128)(2,1)S(1)}, u32[]{:S(2)}, u32[]{:S(2)}) collective-permute-start(bf16[64,3712]{1,0:T(8,128)(2,1)S(1)} %reshape.31), channel_id=1, source_target_pairs={{0,96},{32,0},{64,32},{96,64},{1,97},{33,1},{65,33},{97,65},{2,98}... | collective-permute-start | bytes 1425416 | tf_op jit(solution)/shard_map/ppermute | solution.py:27
  57.1 9.1 %collective-permute-start.5 = (bf16[192,3584]{1,0:T(8,128)(2,1)S(1)}, bf16[192,3584]{1,0:T(8,128)(2,1)S(1)}, u32[]{:S(2)}, u32[]{:S(2)}) collective-permute-start(bf16[192,3584]{1,0:T(8,128)(2,1)S(1)} %pad_maximum_fusion.2), channel_id=1, source_target_pairs={{0,16},{16,0},{1,17},{17,1},{2,18},{18,2},{3,19},{19,3},{4,20},{20... | collective-permute-start | bytes 4128776 | tf_op jit(solution)/shard_map/ppermute | solution.py:31
  58.1 15.4 %collective-permute-start.8 = (bf16[32,3584]{1,0:T(8,128)(2,1)S(1)}, bf16[32,3584]{1,0:T(8,128)(2,1)S(1)}, u32[]{:S(2)}, u32[]{:S(2)}) collective-permute-start(bf16[32,3584]{1,0:T(8,128)(2,1)S(1)} %slice.102), channel_id=1, source_target_pairs={{0,32},{32,64},{64,96},{96,0},{1,33},{33,65},{65,97},{97,1},{2,34}... | collective-permute-start | bytes 688136 | tf_op jit(solution)/shard_map/ppermute | solution.py:27
  59.7 13.9 %collective-permute-start.9 = (bf16[32,3584]{1,0:T(8,128)(2,1)S(1)}, bf16[32,3584]{1,0:T(8,128)(2,1)S(1)}, u32[]{:S(2)}, u32[]{:S(2)}) collective-permute-start(bf16[32,3584]{1,0:T(8,128)(2,1)S(1)} %slice.103), channel_id=1, source_target_pairs={{0,96},{32,0},{64,32},{96,64},{1,97},{33,1},{65,33},{97,65},{2,98}... | collective-permute-start | bytes 688136 | tf_op jit(solution)/shard_map/ppermute | solution.py:27
  63.1 3.8 %copy-start.10 = (bf16[384,3584]{1,0:T(8,128)(2,1)S(1)}, bf16[384,3584]{1,0:T(8,128)(2,1)}, u32[]{:S(2)}) copy-start(bf16[384,3584]{1,0:T(8,128)(2,1)} %get-tuple-element.42) | copy-start | bytes 8257540
  64.2 4.3 %collective-permute-start.2 = (bf16[192,3712]{1,0:T(8,128)(2,1)S(1)}, bf16[192,3712]{1,0:T(8,128)(2,1)S(1)}, u32[]{:S(2)}, u32[]{:S(2)}) collective-permute-start(bf16[192,3712]{1,0:T(8,128)(2,1)S(1)} %pad_maximum_fusion.1), channel_id=1, source_target_pairs={{0,16},{16,0},{1,17},{17,1},{2,18},{18,2},{3,19},{19,3},{4,20},{20... | collective-permute-start | bytes 4276232 | tf_op jit(solution)/shard_map/ppermute | solution.py:31
  64.3 9.2 %collective-permute-start.10 = (bf16[32,3712]{1,0:T(8,128)(2,1)S(1)}, bf16[32,3712]{1,0:T(8,128)(2,1)S(1)}, u32[]{:S(2)}, u32[]{:S(2)}) collective-permute-start(bf16[32,3712]{1,0:T(8,128)(2,1)S(1)} %slice.104), channel_id=1, source_target_pairs={{0,32},{32,64},{64,96},{96,0},{1,33},{33,65},{65,97},{97,1},{2,34}... | collective-permute-start | bytes 712712 | tf_op jit(solution)/shard_map/ppermute | solution.py:27
  66.2 9.4 %collective-permute-start.11 = (bf16[32,3712]{1,0:T(8,128)(2,1)S(1)}, bf16[32,3712]{1,0:T(8,128)(2,1)S(1)}, u32[]{:S(2)}, u32[]{:S(2)}) collective-permute-start(bf16[32,3712]{1,0:T(8,128)(2,1)S(1)} %slice.105), channel_id=1, source_target_pairs={{0,96},{32,0},{64,32},{96,64},{1,97},{33,1},{65,33},{97,65},{2,98}... | collective-permute-start | bytes 712712 | tf_op jit(solution)/shard_map/ppermute | solution.py:27
  75.6 4.4 %collective-permute-start.12 = (bf16[64,3712]{1,0:T(8,128)(2,1)S(1)}, bf16[64,3712]{1,0:T(8,128)(2,1)S(1)}, u32[]{:S(2)}, u32[]{:S(2)}) collective-permute-start(bf16[64,3712]{1,0:T(8,128)(2,1)S(1)} %pad_maximum_fusion.4), channel_id=1, source_target_pairs={{0,16},{16,0},{1,17},{17,1},{2,18},{18,2},{3,19},{19,3},{4,20},{20... | collective-permute-start | bytes 1425416 | tf_op jit(solution)/shard_map/ppermute | solution.py:31
  75.8 2.4 %collective-permute-start.13 = (bf16[64,3584]{1,0:T(8,128)(2,1)S(1)}, bf16[64,3584]{1,0:T(8,128)(2,1)S(1)}, u32[]{:S(2)}, u32[]{:S(2)}) collective-permute-start(bf16[64,3584]{1,0:T(8,128)(2,1)S(1)} %pad_maximum_fusion.6), channel_id=1, source_target_pairs={{0,16},{16,0},{1,17},{17,1},{2,18},{18,2},{3,19},{19,3},{4,20},{20... | collective-permute-start | bytes 1376264 | tf_op jit(solution)/shard_map/ppermute | solution.py:31
  78.3 1.8 %copy-start.4 = (bf16[512,3584]{1,0:T(8,128)(2,1)}, bf16[512,3584]{1,0:T(8,128)(2,1)S(1)}, u32[]{:S(2)}) copy-start(bf16[512,3584]{1,0:T(8,128)(2,1)S(1)} %get-tuple-element.39) | copy-start | bytes 11010052
  80.1 2.6 %copy-start.7 = (bf16[128,3712]{1,0:T(8,128)(2,1)}, bf16[128,3712]{1,0:T(8,128)(2,1)S(1)}, u32[]{:S(2)}) copy-start(bf16[128,3712]{1,0:T(8,128)(2,1)S(1)} %constant_dynamic-update-slice_fusion.8) | copy-start | bytes 2850820
  82.5 1.9 %collective-permute-start.14 = (bf16[64,3712]{1,0:T(8,128)(2,1)S(1)}, bf16[64,3712]{1,0:T(8,128)(2,1)S(1)}, u32[]{:S(2)}, u32[]{:S(2)}) collective-permute-start(bf16[64,3712]{1,0:T(8,128)(2,1)S(1)} %fusion.31), channel_id=1, source_target_pairs={{0,16},{16,0},{1,17},{17,1},{2,18},{18,2},{3,19},{19,3},{4,20},{20... | collective-permute-start | bytes 1425416 | tf_op jit(solution)/shard_map/ppermute | solution.py:31
  83.0 3.7 %collective-permute-start.6 = (bf16[192,3712]{1,0:T(8,128)(2,1)S(1)}, bf16[192,3712]{1,0:T(8,128)(2,1)S(1)}, u32[]{:S(2)}, u32[]{:S(2)}) collective-permute-start(bf16[192,3712]{1,0:T(8,128)(2,1)S(1)} %fusion.8), channel_id=1, source_target_pairs={{0,16},{16,0},{1,17},{17,1},{2,18},{18,2},{3,19},{19,3},{4,20},{20... | collective-permute-start | bytes 4276232 | tf_op jit(solution)/shard_map/ppermute | solution.py:31
  84.6 7.9 %collective-permute-start.15 = (bf16[32,3712]{1,0:T(8,128)(2,1)S(1)}, bf16[32,3712]{1,0:T(8,128)(2,1)S(1)}, u32[]{:S(2)}, u32[]{:S(2)}) collective-permute-start(bf16[32,3712]{1,0:T(8,128)(2,1)S(1)} %get-tuple-element.37), channel_id=1, source_target_pairs={{0,32},{32,64},{64,96},{96,0},{1,33},{33,65},{65,97},{97,1},{2,34}... | collective-permute-start | bytes 712712 | tf_op jit(solution)/shard_map/ppermute | solution.py:27
  85.0 8.8 %collective-permute-start.18 = (bf16[32,3712]{1,0:T(8,128)(2,1)S(1)}, bf16[32,3712]{1,0:T(8,128)(2,1)S(1)}, u32[]{:S(2)}, u32[]{:S(2)}) collective-permute-start(bf16[32,3712]{1,0:T(8,128)(2,1)S(1)} %get-tuple-element.38), channel_id=1, source_target_pairs={{0,96},{32,0},{64,32},{96,64},{1,97},{33,1},{65,33},{97,65},{2,98}... | collective-permute-start | bytes 712712 | tf_op jit(solution)/shard_map/ppermute | solution.py:27
  93.9 8.8 %collective-permute-start.16 = (bf16[32,3712]{1,0:T(8,128)(2,1)S(1)}, bf16[32,3712]{1,0:T(8,128)(2,1)S(1)}, u32[]{:S(2)}, u32[]{:S(2)}) collective-permute-start(bf16[32,3712]{1,0:T(8,128)(2,1)S(1)} %get-tuple-element.27), channel_id=1, source_target_pairs={{0,32},{32,64},{64,96},{96,0},{1,33},{33,65},{65,97},{97,1},{2,34}... | collective-permute-start | bytes 712712 | tf_op jit(solution)/shard_map/ppermute | solution.py:27
  94.2 9.9 %collective-permute-start.19 = (bf16[32,3712]{1,0:T(8,128)(2,1)S(1)}, bf16[32,3712]{1,0:T(8,128)(2,1)S(1)}, u32[]{:S(2)}, u32[]{:S(2)}) collective-permute-start(bf16[32,3712]{1,0:T(8,128)(2,1)S(1)} %get-tuple-element.28), channel_id=1, source_target_pairs={{0,96},{32,0},{64,32},{96,64},{1,97},{33,1},{65,33},{97,65},{2,98}... | collective-permute-start | bytes 712712 | tf_op jit(solution)/shard_map/ppermute | solution.py:27
  96.0 9.7 %collective-permute-start.17 = (bf16[32,3712]{1,0:T(8,128)(2,1)S(1)}, bf16[32,3712]{1,0:T(8,128)(2,1)S(1)}, u32[]{:S(2)}, u32[]{:S(2)}) collective-permute-start(bf16[32,3712]{1,0:T(8,128)(2,1)S(1)} %get-tuple-element.30), channel_id=1, source_target_pairs={{0,32},{32,64},{64,96},{96,0},{1,33},{33,65},{65,97},{97,1},{2,34}... | collective-permute-start | bytes 712712 | tf_op jit(solution)/shard_map/ppermute | solution.py:27
  97.8 9.4 %collective-permute-start.7 = (bf16[32,3712]{1,0:T(8,128)(2,1)S(1)}, bf16[32,3712]{1,0:T(8,128)(2,1)S(1)}, u32[]{:S(2)}, u32[]{:S(2)}) collective-permute-start(bf16[32,3712]{1,0:T(8,128)(2,1)S(1)} %get-tuple-element.29), channel_id=1, source_target_pairs={{0,96},{32,0},{64,32},{96,64},{1,97},{33,1},{65,33},{97,65},{2,98}... | collective-permute-start | bytes 712712 | tf_op jit(solution)/shard_map/ppermute | solution.py:27
  108.4 22.6 %all-to-all-start.2 = ((bf16[32,2,3712]{2,1,0:T(2,128)(2,1)}), bf16[32,2,3712]{2,1,0:T(2,128)(2,1)S(1)}, u32[]{:S(2)}, u32[]{:S(2)}) async-start(bf16[32,2,3712]{2,1,0:T(2,128)(2,1)} %convert_element_type.97), calls=%async_computation.2 | async-start | bytes 950272 | tf_op jit(solution)/shard_map/all_to_all | solution.py:252
  116.7 4.4 %copy-start.5 = (bf16[512,3584]{1,0:T(8,128)(2,1)S(1)}, bf16[512,3584]{1,0:T(8,128)(2,1)}, u32[]{:S(2)}) copy-start(bf16[512,3584]{1,0:T(8,128)(2,1)} %copy-done.4) | copy-start | bytes 11010052
  116.7 4.4 %copy-start.9 = (bf16[128,256]{1,0:T(8,128)(2,1)S(1)}, bf16[128,256]{1,0:T(8,128)(2,1)}, u32[]{:S(2)}) copy-start(bf16[128,256]{1,0:T(8,128)(2,1)} %copy-done.8) | copy-start | bytes 196612
  123.5 7.7 %copy-start.2 = (s32[128,8]{0,1:T(8,128)S(1)}, s32[128,8]{0,1:T(8,128)}, u32[]{:S(2)}) copy-start(s32[128,8]{0,1:T(8,128)} %param.12) | copy-start | bytes 12292
  (3 other events, 3.9 us)

commit v3 on v2

--- a/solution.py
+++ b/solution.py
@@ -121,6 +121,43 @@
     out_ref[:, width:] = tail_ref[...]
 
 
+def work_kernel(n_pieces, *refs):
+    x_pieces, refs = refs[:n_pieces], refs[n_pieces:]
+    pieces = refs[:n_pieces]
+    gate_ref, up_ref, down_ref, mine_ref, twin_ref = refs[n_pieces : n_pieces + 5]
+    act_ref, dh_gate_ref, dh_up_ref, x_ref, dy_ref = refs[n_pieces + 5 :]
+    width = down_ref.shape[2]
+    half = mine_ref.shape[0]
+    first = 0
+    for x_piece, piece in zip(x_pieces, pieces, strict=True):
+        at = pl.ds(first, piece.shape[0])
+        x_ref[at, :] = x_piece[...]
+        dy_ref[at, :] = piece[...]
+        first += piece.shape[0]
+    h_gate = dot(x_ref[...], gate_ref[0], last_pair)
+    h_up = dot(x_ref[...], up_ref[0], last_pair)
+    back = dot(dy_ref[:, :width], down_ref[0], last_pair)
+    weight = dy_ref[:, width : width + 1].astype(F32)
+    sig = jax.nn.sigmoid(h_gate)
+    silu = h_gate * sig
+    act = silu * h_up
+    gate_part = jnp.sum(act * back, axis=1, keepdims=True)
+    d_act = weight * back
+    act_ref[...] = act.astype(BF16)
+    dh_up_ref[...] = (d_act * silu).astype(BF16)
+    dh_gate_ref[...] = (d_act * h_up * sig * (1.0 + h_gate * (1.0 - sig))).astype(BF16)
+    for c in range(0, width, CHUNK):
+        at = pl.ds(c, CHUNK)
+        part = dot(dh_gate_ref[...], gate_ref[0, :, at]) + dot(
+            dh_up_ref[...], up_ref[0, :, at]
+        )
+        mine_ref[:, at] = part[:half].astype(BF16)
+        twin_ref[:, at] = part[half:].astype(BF16)
+    tail = jnp.broadcast_to(gate_part, (2 * half, LANES)).astype(BF16)
+    mine_ref[:, width:] = tail[:half]
+    twin_ref[:, width:] = tail[half:]
+
+
 def home_kernel(home_ref, kept_ref, ids_ref, in_ref, combine_ref):
     width = in_ref.shape[1]
     top, tokens = ids_ref.shape
@@ -201,7 +238,6 @@
             dy, down_rows, last_pair, preferred_element_type=jnp.float32
         )
         gate_part = jnp.sum(act * back, axis=1)
-        scaled = (weight * dy.astype(jnp.float32)).astype(jnp.bfloat16)
         d_act = weight * back
         dh_up = (d_act * h_gate * sig).astype(jnp.bfloat16)
         dh_gate = (d_act * h_up * sig * (1.0 + h_gate * (1.0 - sig))).astype(
@@ -216,27 +252,28 @@
         mine = part[:count] + swap_core(part[count:].astype(jnp.bfloat16)).astype(
             jnp.float32
         )
-        return mine, act.astype(jnp.bfloat16), scaled, dh_gate, dh_up
+        return mine, act.astype(jnp.bfloat16), dh_gate, dh_up
 
     near_x, far_x = spread(send_x)
     near_d, far_d = spread(send_d)
-    near_sum, near_act, near_scaled, near_gate, near_up = work(near_x, near_d)
+    near_sum, near_act, near_gate, near_up = work(near_x, near_d)
     far_x, far_d, _ = lax.optimization_barrier((far_x, far_d, (near_act, near_gate, near_up)))
     far_x, far_d = (jnp.concatenate(v, axis=0) for v in (far_x, far_d))
     far_x, far_d = (jnp.concatenate([v, swap_core(v)], axis=0) for v in (far_x, far_d))
-    far_sum, far_act, far_scaled, far_gate, far_up = work(far_x, far_d)
-
-    def weight_grad(a_near, a_far, b_near, b_far):
-        return lax.dot_general(
-            jnp.concatenate([a_near, a_far], axis=0),
-            jnp.concatenate([b_near, b_far], axis=0),
-            rows_pair,
-            preferred_element_type=jnp.float32,
-        )
-
-    grad_gate = weight_grad(near_gate, far_gate, near_x, far_x)
-    grad_up = weight_grad(near_up, far_up, near_x, far_x)
-    grad_down = weight_grad(near_act, far_act, near_scaled, far_scaled)
+    far_rows = far_x.shape[0]
+    far_mine, far_twin, far_act, far_gate, far_up = call(
+        functools.partial(work_kernel, 1),
+        [((far_rows // 2, wide), BF16)] * 2 + [((far_rows, units), BF16)] * 3,
+        [pltpu.VMEM((far_rows, width), BF16), pltpu.VMEM((far_rows, wide), BF16)],
+        8,
+        (10 * far_rows * width * units, 2 * MIB),
+        far_x,
+        far_d,
+        gate_w,
+        up_w,
+        down_w,
+    )
+    far_sum = far_mine.astype(F32) + swap_core(far_twin).astype(F32)
 
     def send_y(value, step):
         return along_y(value.astype(jnp.bfloat16), step).astype(jnp.float32)
@@ -249,6 +286,24 @@
     low = low + send_y(above_low, 1)
     high = high + send_y(below_high, -1)
     total = jnp.concatenate([low, high], axis=0).astype(jnp.bfloat16)
+    near_d, far_d, _ = lax.optimization_barrier((near_d, far_d, total))
+    near_scaled, far_scaled = (
+        (v[:, width : width + 1].astype(F32) * v[:, :width].astype(F32)).astype(BF16)
+        for v in (near_d, far_d)
+    )
+
+    def weight_grad(a_near, a_far, b_near, b_far):
+        return lax.dot_general(
+            jnp.concatenate([a_near, a_far], axis=0),
+            jnp.concatenate([b_near, b_far], axis=0),
+            rows_pair,
+            preferred_element_type=jnp.float32,
+        )
+
+    grad_gate = weight_grad(near_gate, far_gate, near_x, far_x)
+    grad_up = weight_grad(near_up, far_up, near_x, far_x)
+    grad_down = weight_grad(near_act, far_act, near_scaled, far_scaled)
+
     home = lax.all_to_all(
         total.reshape(groups, CAP, -1), COLUMN, split_axis=0, concat_axis=0, tiled=True
     ).reshape(slots, -1)

time: 133 us -> 131 us (0.985)
  waiting for transfers between devices: 50.9 us -> 58.8 us
  local copies, waits for them, and re-layouts: 13.2 us -> 8.74 us
  matrix products: 18 us -> 13.8 us
  Pallas kernels: 3.42 us -> 6.7 us
  starting transfers between devices: 39.7 us -> 37.4 us
  other arithmetic: 6.17 us -> 4.12 us
    ppermute x14, waiting for transfers between devices: 16.3 us -> 21.1 us  [along_y(): lax.ppermute(value, 'y', [(i, (i + step) % count) for i in range(count)])]
    pallas_call x3 -> x4, Pallas kernels: 3.42 us -> 6.7 us  [call(): pl.pallas_call(kernel, out_shape=out_shape, in_specs=[pl.BlockSpec(memory...]
    reshape x2, local copies, waits for them, and re-layouts: 2.39 us -> 0.35 us  [spread(): own = lax.all_to_all(send.reshape(groups, CAP, wide), COLUMN, split_axis=...]
    all_to_all x2, waiting for transfers between devices: 27.6 us -> 29.2 us  [spread(): lax.all_to_all(send.reshape(groups, CAP, wide), COLUMN, split_axis=0, con...]
    unnamed x35 -> x29, local copies, waits for them, and re-layouts: 6.26 us -> 4.87 us
  transfers between devices with their start and end apart: 23 -> 23, of which waited for: 14 -> 14; matrix products, arithmetic and copies ran while one was open for 23% -> 17% of each run, Pallas kernels for 0% -> 3%
where the time goes in v3:
time: 131 us
  waiting for transfers between devices  58.8 us (45%)
  starting transfers between devices  37.4 us (29%)
  matrix products  13.8 us (11%)
  local copies, waits for them, and re-layouts  8.74 us (7%)
  Pallas kernels  6.7 us (5%)
  other arithmetic  4.12 us (3%)
    all_to_all x2, waiting for transfers between devices, spread(): lax.all_to_all(send.reshape(groups, CAP, wide), COLUMN, split_axis=0, con...  29.2 us
    ppermute x14, waiting for transfers between devices, along_y(): lax.ppermute(value, 'y', [(i, (i + step) % count) for i in range(count)])  21.1 us
    ppermute x14, starting transfers between devices, along_y(): lax.ppermute(value, 'y', [(i, (i + step) % count) for i in range(count)])  15.3 us
    all_to_all x2, starting transfers between devices, spread(): lax.all_to_all(send.reshape(groups, CAP, wide), COLUMN, split_axis=0, con...  15.2 us
    dot_general x3, matrix products, weight_grad(): lax.dot_general(jnp.concatenate([a_near, a_far], axis=0), jnp.concatenate...  9.03 us
    pallas_call x4, Pallas kernels, call(): pl.pallas_call(kernel, out_shape=out_shape, in_specs=[pl.BlockSpec(memory...  6.7 us
    all_to_all x1, waiting for transfers between devices, body(): lax.all_to_all(total.reshape(groups, CAP, -1), COLUMN, split_axis=0, conc...  6.42 us
    all_to_all x1, starting transfers between devices, body(): lax.all_to_all(total.reshape(groups, CAP, -1), COLUMN, split_axis=0, conc...  5.73 us
  transfers between devices with their start and end apart: 23, of which 14 were waited for; matrix products, arithmetic and copies ran while one was open for 17% of the time, Pallas kernels for 3%

profile of v3, /device:TPU:24, one launch (start us, length us, event | category | flops | bytes accessed | tf_op | source)
XLA Modules:
  0.0 130.6 jit_solution(3982923389435783643)
XLA Ops:
  0.6 1.7 %shard_map.119 = (bf16[64,3584]{1,0:T(8,128)(2,1)S(1)}, bf16[64,128]{1,0:T(8,128)(2,1)S(1)}, bf16[64,128]{1,0:T(8,128)(2,1)S(1)}) custom-call(s32[8,128]{1,0:T(8,128)} %bitcast.31, bf16[8,128]{1,0:T(8,128)(2,1)} %bitcast.34, bf16[28,128]{1,0:T(8,128)(2,1)} %bitcast.33, bf16[128,3584]{1,0:T(8,128)(2,1)} %refs_3_.2), custom_call_target="tpu_custom_call" | custom-call | flops 58720256 | bytes 1048576 | tf_op jit(solution)/shard_map/pallas_call | solution.py:44
  3.3 11.3 %all-to-all-start.1 = ((bf16[32,2,3584]{2,1,0:T(2,128)(2,1)}), bf16[32,2,3584]{2,1,0:T(2,128)(2,1)S(1)}, u32[]{:S(2)}, u32[]{:S(2)}) async-start(bf16[32,2,3584]{2,1,0:T(2,128)(2,1)} %reshape.31), calls=%async_computation.1 | async-start | bytes 917504 | tf_op jit(solution)/shard_map/all_to_all | solution.py:209
  15.9 15.9 %all-to-all-done.1 = bf16[32,2,3584]{2,1,0:T(2,128)(2,1)S(1)} async-done(((bf16[32,2,3584]{2,1,0:T(2,128)(2,1)}), bf16[32,2,3584]{2,1,0:T(2,128)(2,1)S(1)}, u32[]{:S(2)}, u32[]{:S(2)}) %all-to-all-start.1) | async-done | bytes 458784 | tf_op jit(solution)/shard_map/all_to_all | solution.py:209
  31.7 3.9 %all-to-all-start = ((bf16[32,2,3712]{2,1,0:T(2,128)(2,1)}), bf16[32,2,3712]{2,1,0:T(2,128)(2,1)S(1)}, u32[]{:S(2)}, u32[]{:S(2)}) async-start(bf16[32,2,3712]{2,1,0:T(2,128)(2,1)} %reshape.29), calls=%async_computation | async-start | bytes 950272 | tf_op jit(solution)/shard_map/all_to_all | solution.py:209
  36.1 1.8 %collective-permute-start.4 = (bf16[64,3584]{1,0:T(8,128)(2,1)S(1)}, bf16[64,3584]{1,0:T(8,128)(2,1)S(1)}, u32[]{:S(2)}, u32[]{:S(2)}) collective-permute-start(bf16[64,3584]{1,0:T(8,128)(2,1)S(1)} %reshape.32), channel_id=1, source_target_pairs={{0,96},{32,0},{64,32},{96,64},{1,97},{33,1},{65,33},{97,65},{2,98}... | collective-permute-start | bytes 1376264 | tf_op jit(solution)/shard_map/ppermute | solution.py:27
  38.9 13.4 %all-to-all-done = bf16[32,2,3712]{2,1,0:T(2,128)(2,1)S(1)} async-done(((bf16[32,2,3712]{2,1,0:T(2,128)(2,1)}), bf16[32,2,3712]{2,1,0:T(2,128)(2,1)S(1)}, u32[]{:S(2)}, u32[]{:S(2)}) %all-to-all-start) | async-done | bytes 475168 | tf_op jit(solution)/shard_map/all_to_all | solution.py:209
  52.8 1.8 %collective-permute-start.1 = (bf16[64,3712]{1,0:T(8,128)(2,1)S(1)}, bf16[64,3712]{1,0:T(8,128)(2,1)S(1)}, u32[]{:S(2)}, u32[]{:S(2)}) collective-permute-start(bf16[64,3712]{1,0:T(8,128)(2,1)S(1)} %reshape.30), channel_id=1, source_target_pairs={{0,96},{32,0},{64,32},{96,64},{1,97},{33,1},{65,33},{97,65},{2,98}... | collective-permute-start | bytes 1425416 | tf_op jit(solution)/shard_map/ppermute | solution.py:27
  54.9 1.5 %collective-permute-start.8 = (bf16[32,3584]{1,0:T(8,128)(2,1)S(1)}, bf16[32,3584]{1,0:T(8,128)(2,1)S(1)}, u32[]{:S(2)}, u32[]{:S(2)}) collective-permute-start(bf16[32,3584]{1,0:T(8,128)(2,1)S(1)} %slice.101), channel_id=1, source_target_pairs={{0,32},{32,64},{64,96},{96,0},{1,33},{33,65},{65,97},{97,1},{2,34}... | collective-permute-start | bytes 688136 | tf_op jit(solution)/shard_map/ppermute | solution.py:27
  58.8 5.5 %collective-permute-done = bf16[64,3712]{1,0:T(8,128)(2,1)S(1)} collective-permute-done((bf16[64,3712]{1,0:T(8,128)(2,1)S(1)}, bf16[64,3712]{1,0:T(8,128)(2,1)S(1)}, u32[]{:S(2)}, u32[]{:S(2)}) %collective-permute-start) | collective-permute-done | bytes 475168 | tf_op jit(solution)/shard_map/ppermute | solution.py:27
  64.2 1.3 collective-permute-done.1
  66.2 2.1 %collective-permute-start.11 = (bf16[32,3712]{1,0:T(8,128)(2,1)S(1)}, bf16[32,3712]{1,0:T(8,128)(2,1)S(1)}, u32[]{:S(2)}, u32[]{:S(2)}) collective-permute-start(bf16[32,3712]{1,0:T(8,128)(2,1)S(1)} %slice.104), channel_id=1, source_target_pairs={{0,96},{32,0},{64,32},{96,64},{1,97},{33,1},{65,33},{97,65},{2,98}... | collective-permute-start | bytes 712712 | tf_op jit(solution)/shard_map/ppermute | solution.py:27
  69.7 1.2 copy-done.2
  72.4 1.1 multiply_convert_fusion.3
  74.5 1.2 collective-permute-done.11
  78.4 3.4 %shard_map.121 = (bf16[64,3712]{1,0:T(8,128)(2,1)S(1)}, bf16[64,3712]{1,0:T(8,128)(2,1)S(1)}, bf16[128,256]{1,0:T(8,128)(2,1)S(1)}, bf16[128,256]{1,0:T(8,128)(2,1)S(1)}, bf16[128,256]{1,0:T(8,128)(2,1)S(1)}) custom-call(bf16[128,3584]{1,0:T(8,128)(2,1)S(1)} %pad_maximum_fusion.3.refs_0_, bf16[128,3712]{1,0:T(8,128)(2,1)S(1)} %constant_dynamic-update-slice_fusion.8.refs_1_, ...), custom_call_target="tpu_custom_call" | custom-call | flops 1174405120 | bytes 2097152 | tf_op jit(solution)/shard_map/pallas_call | solution.py:44
  82.2 1.5 %collective-permute-done.14 = bf16[64,3712]{1,0:T(8,128)(2,1)S(1)} collective-permute-done((bf16[64,3712]{1,0:T(8,128)(2,1)S(1)}, bf16[64,3712]{1,0:T(8,128)(2,1)S(1)}, u32[]{:S(2)}, u32[]{:S(2)}) %collective-permute-start.14) | collective-permute-done | bytes 475168 | tf_op jit(solution)/shard_map/ppermute | solution.py:31
  84.3 1.7 %collective-permute-start.18 = (bf16[32,3712]{1,0:T(8,128)(2,1)S(1)}, bf16[32,3712]{1,0:T(8,128)(2,1)S(1)}, u32[]{:S(2)}, u32[]{:S(2)}) collective-permute-start(bf16[32,3712]{1,0:T(8,128)(2,1)S(1)} %get-tuple-element.52), channel_id=1, source_target_pairs={{0,96},{32,0},{64,32},{96,64},{1,97},{33,1},{65,33},{97,65},{2,98}... | collective-permute-start | bytes 712712 | tf_op jit(solution)/shard_map/ppermute | solution.py:27
  86.3 5.5 %collective-permute-done.15 = bf16[32,3712]{1,0:T(8,128)(2,1)S(1)} collective-permute-done((bf16[32,3712]{1,0:T(8,128)(2,1)S(1)}, bf16[32,3712]{1,0:T(8,128)(2,1)S(1)}, u32[]{:S(2)}, u32[]{:S(2)}) %collective-permute-start.15) | collective-permute-done | bytes 237600 | tf_op jit(solution)/shard_map/ppermute | solution.py:27
  91.8 1.3 collective-permute-done.18
  93.5 1.8 %collective-permute-start.19 = (bf16[32,3712]{1,0:T(8,128)(2,1)S(1)}, bf16[32,3712]{1,0:T(8,128)(2,1)S(1)}, u32[]{:S(2)}, u32[]{:S(2)}) collective-permute-start(bf16[32,3712]{1,0:T(8,128)(2,1)S(1)} %get-tuple-element.42), channel_id=1, source_target_pairs={{0,96},{32,0},{64,32},{96,64},{1,97},{33,1},{65,33},{97,65},{2,98}... | collective-permute-start | bytes 712712 | tf_op jit(solution)/shard_map/ppermute | solution.py:27
  95.3 1.7 %collective-permute-start.17 = (bf16[32,3712]{1,0:T(8,128)(2,1)S(1)}, bf16[32,3712]{1,0:T(8,128)(2,1)S(1)}, u32[]{:S(2)}, u32[]{:S(2)}) collective-permute-start(bf16[32,3712]{1,0:T(8,128)(2,1)S(1)} %get-tuple-element.44), channel_id=1, source_target_pairs={{0,32},{32,64},{64,96},{96,0},{1,33},{33,65},{65,97},{97,1},{2,34}... | collective-permute-start | bytes 712712 | tf_op jit(solution)/shard_map/ppermute | solution.py:27
  97.7 2.4 %multiply_convert_fusion = bf16[384,3584]{1,0:T(8,128)(2,1)} fusion(bf16[384,3712]{1,0:T(8,128)(2,1)S(1)} %constant_dynamic-update-slice_fusion, f32[384]{0:T(512)S(1)} %convert_reduce_fusion), kind=kLoop, calls=%fused_computation.3 | loop fusion | flops 4128768 | bytes 5506560 | tf_op jit(solution)/shard_map/convert_element_type | solution.py:291
  100.2 1.8 %collective-permute-done.16 = bf16[32,3712]{1,0:T(8,128)(2,1)S(1)} collective-permute-done((bf16[32,3712]{1,0:T(8,128)(2,1)S(1)}, bf16[32,3712]{1,0:T(8,128)(2,1)S(1)}, u32[]{:S(2)}, u32[]{:S(2)}) %collective-permute-start.16) | collective-permute-done | bytes 237600 | tf_op jit(solution)/shard_map/ppermute | solution.py:27
  102.0 1.4 %collective-permute-done.19 = bf16[32,3712]{1,0:T(8,128)(2,1)S(1)} collective-permute-done((bf16[32,3712]{1,0:T(8,128)(2,1)S(1)}, bf16[32,3712]{1,0:T(8,128)(2,1)S(1)}, u32[]{:S(2)}, u32[]{:S(2)}) %collective-permute-start.19) | collective-permute-done | bytes 237600 | tf_op jit(solution)/shard_map/ppermute | solution.py:27
  103.4 1.7 %collective-permute-done.17 = bf16[32,3712]{1,0:T(8,128)(2,1)S(1)} collective-permute-done((bf16[32,3712]{1,0:T(8,128)(2,1)S(1)}, bf16[32,3712]{1,0:T(8,128)(2,1)S(1)}, u32[]{:S(2)}, u32[]{:S(2)}) %collective-permute-start.17) | collective-permute-done | bytes 237600 | tf_op jit(solution)/shard_map/ppermute | solution.py:27
  105.1 1.4 %collective-permute-done.7 = bf16[32,3712]{1,0:T(8,128)(2,1)S(1)} collective-permute-done((bf16[32,3712]{1,0:T(8,128)(2,1)S(1)}, bf16[32,3712]{1,0:T(8,128)(2,1)S(1)}, u32[]{:S(2)}, u32[]{:S(2)}) %collective-permute-start.7) | collective-permute-done | bytes 237600 | tf_op jit(solution)/shard_map/ppermute | solution.py:27
  107.7 5.7 %all-to-all-start.2 = ((bf16[32,2,3712]{2,1,0:T(2,128)(2,1)}), bf16[32,2,3712]{2,1,0:T(2,128)(2,1)S(1)}, u32[]{:S(2)}, u32[]{:S(2)}) async-start(bf16[32,2,3712]{2,1,0:T(2,128)(2,1)} %convert_element_type.90), calls=%async_computation.2 | async-start | bytes 950272 | tf_op jit(solution)/shard_map/all_to_all | solution.py:307
  113.6 4.3 %fusion.2 = bf16[1,256,3584]{2,1,0:T(8,128)(2,1)} fusion(bf16[128,3584]{1,0:T(8,128)(2,1)S(1)} %multiply_convert_fusion.1, bf16[384,3584]{1,0:T(8,128)(2,1)} %multiply_convert_fusion, bf16[128,256]{1,0:T(8,128)(2,1)S(1)} %get-tuple-element.34, bf16[384,256]{1,0:T(8,128)(2,1)S(1)} %get-tuple-element.50), kind=kOutput, calls=%fused_computation.9 | convolution fusion | flops 948305920 | bytes 5767168 | tf_op jit(solution)/shard_map/dot_general | solution.py:296
  117.9 2.4 %fusion.1 = bf16[1,256,3584]{2,1,0:T(8,128)(2,1)} fusion(bf16[512,3584]{1,0:T(8,128)(2,1)S(1)} %copy-done.7, bf16[128,256]{1,0:T(8,128)(2,1)S(1)} %get-tuple-element.33, bf16[384,256]{1,0:T(8,128)(2,1)S(1)} %get-tuple-element.49), kind=kOutput, calls=%fused_computation.8 | convolution fusion | flops 940965888 | bytes 5767168 | tf_op jit(solution)/shard_map/dot_general | solution.py:296
  120.3 2.4 %fusion = bf16[1,256,3584]{2,1,0:T(8,128)(2,1)} fusion(bf16[512,3584]{1,0:T(8,128)(2,1)S(1)} %copy-done.7, bf16[128,256]{1,0:T(8,128)(2,1)S(1)} %get-tuple-element.32, bf16[384,256]{1,0:T(8,128)(2,1)S(1)} %get-tuple-element.47), kind=kOutput, calls=%fused_computation.7 | convolution fusion | flops 940965888 | bytes 5767168 | tf_op jit(solution)/shard_map/dot_general | solution.py:296
  122.7 6.4 %all-to-all-done.2 = bf16[32,2,3712]{2,1,0:T(2,128)(2,1)S(1)} async-done(((bf16[32,2,3712]{2,1,0:T(2,128)(2,1)}), bf16[32,2,3712]{2,1,0:T(2,128)(2,1)S(1)}, u32[]{:S(2)}, u32[]{:S(2)}) %all-to-all-start.2) | async-done | bytes 475168 | tf_op jit(solution)/shard_map/all_to_all | solution.py:307
  129.3 1.3 %shard_map.122 = (bf16[128,3584]{1,0:T(8,128)(2,1)}, bf16[8,128]{1,0:T(8,128)(2,1)}) custom-call(bf16[64,3712]{1,0:T(8,128)(2,1)S(1)} %reshape.33.home_ref, bf16[64,128]{1,0:T(8,128)(2,1)S(1)} %get-tuple-element.21.kept_ref, s32[8,128]{1,0:T(8,128)S(1)} %bitcast.32), custom_call_target="tpu_custom_call" | custom-call | flops 58720256 | bytes 2097152 | tf_op jit(solution)/shard_map/pallas_call | solution.py:44
  (87 shorter events, 17.7 us)
Async XLA Ops:
  0.6 14.0 %copy-start.3 = (bf16[128,3584]{1,0:T(8,128)(2,1)S(1)}, bf16[128,3584]{1,0:T(8,128)(2,1)}, u32[]{:S(2)}) copy-start(bf16[128,3584]{1,0:T(8,128)(2,1)} %dy_ref.1) | copy-start | bytes 2752516
  3.3 28.4 %all-to-all-start.1 = ((bf16[32,2,3584]{2,1,0:T(2,128)(2,1)}), bf16[32,2,3584]{2,1,0:T(2,128)(2,1)S(1)}, u32[]{:S(2)}, u32[]{:S(2)}) async-start(bf16[32,2,3584]{2,1,0:T(2,128)(2,1)} %reshape.31), calls=%async_computation.1 | async-start | bytes 917504 | tf_op jit(solution)/shard_map/all_to_all | solution.py:209
  31.7 20.6 %all-to-all-start = ((bf16[32,2,3712]{2,1,0:T(2,128)(2,1)}), bf16[32,2,3712]{2,1,0:T(2,128)(2,1)S(1)}, u32[]{:S(2)}, u32[]{:S(2)}) async-start(bf16[32,2,3712]{2,1,0:T(2,128)(2,1)} %reshape.29), calls=%async_computation | async-start | bytes 950272 | tf_op jit(solution)/shard_map/all_to_all | solution.py:209
  35.8 18.8 %collective-permute-start.3 = (bf16[64,3584]{1,0:T(8,128)(2,1)S(1)}, bf16[64,3584]{1,0:T(8,128)(2,1)S(1)}, u32[]{:S(2)}, u32[]{:S(2)}) collective-permute-start(bf16[64,3584]{1,0:T(8,128)(2,1)S(1)} %reshape.32), channel_id=1, source_target_pairs={{0,32},{32,64},{64,96},{96,0},{1,33},{33,65},{65,97},{97,1},{2,34}... | collective-permute-start | bytes 1376264 | tf_op jit(solution)/shard_map/ppermute | solution.py:27
  36.1 18.5 %collective-permute-start.4 = (bf16[64,3584]{1,0:T(8,128)(2,1)S(1)}, bf16[64,3584]{1,0:T(8,128)(2,1)S(1)}, u32[]{:S(2)}, u32[]{:S(2)}) collective-permute-start(bf16[64,3584]{1,0:T(8,128)(2,1)S(1)} %reshape.32), channel_id=1, source_target_pairs={{0,96},{32,0},{64,32},{96,64},{1,97},{33,1},{65,33},{97,65},{2,98}... | collective-permute-start | bytes 1376264 | tf_op jit(solution)/shard_map/ppermute | solution.py:27
  52.5 4.6 %copy-start.5 = (bf16[512,3584]{1,0:T(8,128)(2,1)S(1)}, bf16[512,3584]{1,0:T(8,128)(2,1)}, u32[]{:S(2)}) copy-start(bf16[512,3584]{1,0:T(8,128)(2,1)} %get-tuple-element.57) | copy-start | bytes 11010052
  52.5 11.8 %collective-permute-start = (bf16[64,3712]{1,0:T(8,128)(2,1)S(1)}, bf16[64,3712]{1,0:T(8,128)(2,1)S(1)}, u32[]{:S(2)}, u32[]{:S(2)}) collective-permute-start(bf16[64,3712]{1,0:T(8,128)(2,1)S(1)} %reshape.30), channel_id=1, source_target_pairs={{0,32},{32,64},{64,96},{96,0},{1,33},{33,65},{65,97},{97,1},{2,34}... | collective-permute-start | bytes 1425416 | tf_op jit(solution)/shard_map/ppermute | solution.py:27
  52.8 12.8 %collective-permute-start.1 = (bf16[64,3712]{1,0:T(8,128)(2,1)S(1)}, bf16[64,3712]{1,0:T(8,128)(2,1)S(1)}, u32[]{:S(2)}, u32[]{:S(2)}) collective-permute-start(bf16[64,3712]{1,0:T(8,128)(2,1)S(1)} %reshape.30), channel_id=1, source_target_pairs={{0,96},{32,0},{64,32},{96,64},{1,97},{33,1},{65,33},{97,65},{2,98}... | collective-permute-start | bytes 1425416 | tf_op jit(solution)/shard_map/ppermute | solution.py:27
  54.7 11.5 %collective-permute-start.5 = (bf16[192,3584]{1,0:T(8,128)(2,1)S(1)}, bf16[192,3584]{1,0:T(8,128)(2,1)S(1)}, u32[]{:S(2)}, u32[]{:S(2)}) collective-permute-start(bf16[192,3584]{1,0:T(8,128)(2,1)S(1)} %pad_maximum_fusion.2), channel_id=1, source_target_pairs={{0,16},{16,0},{1,17},{17,1},{2,18},{18,2},{3,19},{19,3},{4,20},{20... | collective-permute-start | bytes 4128776 | tf_op jit(solution)/shard_map/ppermute | solution.py:31
  54.9 19.6 %collective-permute-start.8 = (bf16[32,3584]{1,0:T(8,128)(2,1)S(1)}, bf16[32,3584]{1,0:T(8,128)(2,1)S(1)}, u32[]{:S(2)}, u32[]{:S(2)}) collective-permute-start(bf16[32,3584]{1,0:T(8,128)(2,1)S(1)} %slice.101), channel_id=1, source_target_pairs={{0,32},{32,64},{64,96},{96,0},{1,33},{33,65},{65,97},{97,1},{2,34}... | collective-permute-start | bytes 688136 | tf_op jit(solution)/shard_map/ppermute | solution.py:27
  56.4 18.0 %collective-permute-start.9 = (bf16[32,3584]{1,0:T(8,128)(2,1)S(1)}, bf16[32,3584]{1,0:T(8,128)(2,1)S(1)}, u32[]{:S(2)}, u32[]{:S(2)}) collective-permute-start(bf16[32,3584]{1,0:T(8,128)(2,1)S(1)} %slice.102), channel_id=1, source_target_pairs={{0,96},{32,0},{64,32},{96,64},{1,97},{33,1},{65,33},{97,65},{2,98}... | collective-permute-start | bytes 688136 | tf_op jit(solution)/shard_map/ppermute | solution.py:27
  58.8 9.5 %copy-start.8 = (bf16[384,3584]{1,0:T(8,128)(2,1)S(1)}, bf16[384,3584]{1,0:T(8,128)(2,1)}, u32[]{:S(2)}) copy-start(bf16[384,3584]{1,0:T(8,128)(2,1)} %get-tuple-element.54) | copy-start | bytes 8257540
  65.7 3.7 %collective-permute-start.2 = (bf16[192,3712]{1,0:T(8,128)(2,1)S(1)}, bf16[192,3712]{1,0:T(8,128)(2,1)S(1)}, u32[]{:S(2)}, u32[]{:S(2)}) collective-permute-start(bf16[192,3712]{1,0:T(8,128)(2,1)S(1)} %pad_maximum_fusion.1), channel_id=1, source_target_pairs={{0,16},{16,0},{1,17},{17,1},{2,18},{18,2},{3,19},{19,3},{4,20},{20... | collective-permute-start | bytes 4276232 | tf_op jit(solution)/shard_map/ppermute | solution.py:31
  65.8 8.7 %collective-permute-start.10 = (bf16[32,3712]{1,0:T(8,128)(2,1)S(1)}, bf16[32,3712]{1,0:T(8,128)(2,1)S(1)}, u32[]{:S(2)}, u32[]{:S(2)}) collective-permute-start(bf16[32,3712]{1,0:T(8,128)(2,1)S(1)} %slice.103), channel_id=1, source_target_pairs={{0,32},{32,64},{64,96},{96,0},{1,33},{33,65},{65,97},{97,1},{2,34}... | collective-permute-start | bytes 712712 | tf_op jit(solution)/shard_map/ppermute | solution.py:27
  66.1 2.4 %copy-start.1 = (bf16[1,256,3584]{2,1,0:T(8,128)(2,1)S(1)}, bf16[1,256,3584]{2,1,0:T(8,128)(2,1)}, u32[]{:S(2)}) copy-start(bf16[1,256,3584]{2,1,0:T(8,128)(2,1)} %refs_3_.3) | copy-start | bytes 5505028
  66.2 9.4 %collective-permute-start.11 = (bf16[32,3712]{1,0:T(8,128)(2,1)S(1)}, bf16[32,3712]{1,0:T(8,128)(2,1)S(1)}, u32[]{:S(2)}, u32[]{:S(2)}) collective-permute-start(bf16[32,3712]{1,0:T(8,128)(2,1)S(1)} %slice.104), channel_id=1, source_target_pairs={{0,96},{32,0},{64,32},{96,64},{1,97},{33,1},{65,33},{97,65},{2,98}... | collective-permute-start | bytes 712712 | tf_op jit(solution)/shard_map/ppermute | solution.py:27
  69.4 1.5 %copy-start.2 = (bf16[1,256,3584]{2,1,0:T(8,128)(2,1)S(1)}, bf16[1,256,3584]{2,1,0:T(8,128)(2,1)}, u32[]{:S(2)}) copy-start(bf16[1,256,3584]{2,1,0:T(8,128)(2,1)} %refs_4_.1) | copy-start | bytes 5505028
  70.9 1.5 %copy-start = (bf16[1,256,3584]{2,1,0:T(8,128)(2,1)S(1)}, bf16[1,256,3584]{2,1,0:T(8,128)(2,1)}, u32[]{:S(2)}) copy-start(bf16[1,256,3584]{2,1,0:T(8,128)(2,1)} %refs_2_.1) | copy-start | bytes 5505028
  75.7 2.6 %collective-permute-start.13 = (bf16[64,3712]{1,0:T(8,128)(2,1)S(1)}, bf16[64,3712]{1,0:T(8,128)(2,1)S(1)}, u32[]{:S(2)}, u32[]{:S(2)}) collective-permute-start(bf16[64,3712]{1,0:T(8,128)(2,1)S(1)} %pad_maximum_fusion.4), channel_id=1, source_target_pairs={{0,16},{16,0},{1,17},{17,1},{2,18},{18,2},{3,19},{19,3},{4,20},{20... | collective-permute-start | bytes 1425416 | tf_op jit(solution)/shard_map/ppermute | solution.py:31
  75.9 2.4 %collective-permute-start.12 = (bf16[64,3584]{1,0:T(8,128)(2,1)S(1)}, bf16[64,3584]{1,0:T(8,128)(2,1)S(1)}, u32[]{:S(2)}, u32[]{:S(2)}) collective-permute-start(bf16[64,3584]{1,0:T(8,128)(2,1)S(1)} %pad_maximum_fusion.6), channel_id=1, source_target_pairs={{0,16},{16,0},{1,17},{17,1},{2,18},{18,2},{3,19},{19,3},{4,20},{20... | collective-permute-start | bytes 1376264 | tf_op jit(solution)/shard_map/ppermute | solution.py:31
  77.7 8.3 %collective-permute-start.6 = (bf16[192,3712]{1,0:T(8,128)(2,1)S(1)}, bf16[192,3712]{1,0:T(8,128)(2,1)S(1)}, u32[]{:S(2)}, u32[]{:S(2)}) collective-permute-start(bf16[192,3712]{1,0:T(8,128)(2,1)S(1)} %fusion.8), channel_id=1, source_target_pairs={{0,16},{16,0},{1,17},{17,1},{2,18},{18,2},{3,19},{19,3},{4,20},{20... | collective-permute-start | bytes 4276232 | tf_op jit(solution)/shard_map/ppermute | solution.py:31
  81.8 1.9 %collective-permute-start.14 = (bf16[64,3712]{1,0:T(8,128)(2,1)S(1)}, bf16[64,3712]{1,0:T(8,128)(2,1)S(1)}, u32[]{:S(2)}, u32[]{:S(2)}) collective-permute-start(bf16[64,3712]{1,0:T(8,128)(2,1)S(1)} %get-tuple-element.29), channel_id=1, source_target_pairs={{0,16},{16,0},{1,17},{17,1},{2,18},{18,2},{3,19},{19,3},{4,20},{20... | collective-permute-start | bytes 1425416 | tf_op jit(solution)/shard_map/ppermute | solution.py:31
  82.1 4.2 %copy-start.6 = (bf16[512,3584]{1,0:T(8,128)(2,1)}, bf16[512,3584]{1,0:T(8,128)(2,1)S(1)}, u32[]{:S(2)}) copy-start(bf16[512,3584]{1,0:T(8,128)(2,1)S(1)} %constant_dynamic-update-slice_fusion.11) | copy-start | bytes 11010052
  83.9 7.9 %collective-permute-start.15 = (bf16[32,3712]{1,0:T(8,128)(2,1)S(1)}, bf16[32,3712]{1,0:T(8,128)(2,1)S(1)}, u32[]{:S(2)}, u32[]{:S(2)}) collective-permute-start(bf16[32,3712]{1,0:T(8,128)(2,1)S(1)} %get-tuple-element.51), channel_id=1, source_target_pairs={{0,32},{32,64},{64,96},{96,0},{1,33},{33,65},{65,97},{97,1},{2,34}... | collective-permute-start | bytes 712712 | tf_op jit(solution)/shard_map/ppermute | solution.py:27
  84.3 8.8 %collective-permute-start.18 = (bf16[32,3712]{1,0:T(8,128)(2,1)S(1)}, bf16[32,3712]{1,0:T(8,128)(2,1)S(1)}, u32[]{:S(2)}, u32[]{:S(2)}) collective-permute-start(bf16[32,3712]{1,0:T(8,128)(2,1)S(1)} %get-tuple-element.52), channel_id=1, source_target_pairs={{0,96},{32,0},{64,32},{96,64},{1,97},{33,1},{65,33},{97,65},{2,98}... | collective-permute-start | bytes 712712 | tf_op jit(solution)/shard_map/ppermute | solution.py:27
  93.2 8.8 %collective-permute-start.16 = (bf16[32,3712]{1,0:T(8,128)(2,1)S(1)}, bf16[32,3712]{1,0:T(8,128)(2,1)S(1)}, u32[]{:S(2)}, u32[]{:S(2)}) collective-permute-start(bf16[32,3712]{1,0:T(8,128)(2,1)S(1)} %get-tuple-element.41), channel_id=1, source_target_pairs={{0,32},{32,64},{64,96},{96,0},{1,33},{33,65},{65,97},{97,1},{2,34}... | collective-permute-start | bytes 712712 | tf_op jit(solution)/shard_map/ppermute | solution.py:27
  93.5 9.9 %collective-permute-start.19 = (bf16[32,3712]{1,0:T(8,128)(2,1)S(1)}, bf16[32,3712]{1,0:T(8,128)(2,1)S(1)}, u32[]{:S(2)}, u32[]{:S(2)}) collective-permute-start(bf16[32,3712]{1,0:T(8,128)(2,1)S(1)} %get-tuple-element.42), channel_id=1, source_target_pairs={{0,96},{32,0},{64,32},{96,64},{1,97},{33,1},{65,33},{97,65},{2,98}... | collective-permute-start | bytes 712712 | tf_op jit(solution)/shard_map/ppermute | solution.py:27
  95.3 9.8 %collective-permute-start.17 = (bf16[32,3712]{1,0:T(8,128)(2,1)S(1)}, bf16[32,3712]{1,0:T(8,128)(2,1)S(1)}, u32[]{:S(2)}, u32[]{:S(2)}) collective-permute-start(bf16[32,3712]{1,0:T(8,128)(2,1)S(1)} %get-tuple-element.44), channel_id=1, source_target_pairs={{0,32},{32,64},{64,96},{96,0},{1,33},{33,65},{65,97},{97,1},{2,34}... | collective-permute-start | bytes 712712 | tf_op jit(solution)/shard_map/ppermute | solution.py:27
  97.1 9.4 %collective-permute-start.7 = (bf16[32,3712]{1,0:T(8,128)(2,1)S(1)}, bf16[32,3712]{1,0:T(8,128)(2,1)S(1)}, u32[]{:S(2)}, u32[]{:S(2)}) collective-permute-start(bf16[32,3712]{1,0:T(8,128)(2,1)S(1)} %get-tuple-element.43), channel_id=1, source_target_pairs={{0,96},{32,0},{64,32},{96,64},{1,97},{33,1},{65,33},{97,65},{2,98}... | collective-permute-start | bytes 712712 | tf_op jit(solution)/shard_map/ppermute | solution.py:27
  107.7 21.4 %all-to-all-start.2 = ((bf16[32,2,3712]{2,1,0:T(2,128)(2,1)}), bf16[32,2,3712]{2,1,0:T(2,128)(2,1)S(1)}, u32[]{:S(2)}, u32[]{:S(2)}) async-start(bf16[32,2,3712]{2,1,0:T(2,128)(2,1)} %convert_element_type.90), calls=%async_computation.2 | async-start | bytes 950272 | tf_op jit(solution)/shard_map/all_to_all | solution.py:307
  113.6 4.3 %copy-start.7 = (bf16[512,3584]{1,0:T(8,128)(2,1)S(1)}, bf16[512,3584]{1,0:T(8,128)(2,1)}, u32[]{:S(2)}) copy-start(bf16[512,3584]{1,0:T(8,128)(2,1)} %copy-done.6) | copy-start | bytes 11010052
  120.3 9.0 %copy-start.4 = (s32[128,8]{0,1:T(8,128)S(1)}, s32[128,8]{0,1:T(8,128)}, u32[]{:S(2)}) copy-start(s32[128,8]{0,1:T(8,128)} %param.12) | copy-start | bytes 12292
